TPU v7x, 128 devices: a whole 4x4x4 slice. The times are simulated.
128 devices in a mesh: section: 8 (over x_hi, y), dp: 16 (over z, x_lo, core).
Axes of the slice: x: 4 (x_hi: 2, x_lo: 2; x = x_hi * 2 + x_lo), y: 4, z: 4, core: 2. Of those that a mesh axis runs over, the one named last changes fastest.
Arguments:
- state: bfloat16 [8, 256, 3072], P(None, 'dp'), may hold values from -17 to 17
- adjoint: bfloat16 [8, 256, 3072], P(None, 'dp'), may hold values from -6 to 6
- probe: int32 [8, 256, 3072], P(None, 'dp'), may hold values from -1 to 1, as said below
- logp: float32 [8, 16], P(None, 'dp'), may hold values from -6 to 6
- density_weight: float32 [8, 16], P(None, 'dp'), may hold values from 0.5 to 1.5
- step_size: float32 [1], replicated, may hold values from 0.2 to 0.5
- norm_gain: float32 [8, 3072], P('section'), may hold values from 0.25 to 1.75
- norm_shift: float32 [8, 3072], P('section'), may hold values from -3 to 3
- branch_gate: float32 [8, 3072], P('section'), may hold values from 0.4 to 1.2
- weights: bfloat16 [8, 3072, 3072], P('section'), may hold values from -1 to 1
Outputs:
- state_next: float32 [8, 256, 3072], P('section', 'dp')
- adjoint_next: float32 [8, 256, 3072], P('section', 'dp')
- logp_next: float32 [8, 16], P('section', 'dp')
- weight_grad: float32 [8, 3072, 3072], P('section', 'dp')
Inputs may be any that keep to these rules, and one draw needn't show every extreme that they name: `probe`: every entry is -1 or +1.
All inputs are finite; a program needn't handle non-finite values.
Results may differ from a plain program's by a relative error of at most 0.022.
Values may be sent and summed in bfloat16 or wider, within the bound.
A program may use at most 192 MiB of HBM per device.

v0:
```python
import jax
import jax.numpy as jnp
from jax import lax
from jax.sharding import PartitionSpec as P

EPSILON = 1e-06


def passed_along(value, axis, steps):
    count = lax.axis_size(axis)
    first, last = (max(0, -steps), min(count, count - steps))
    return lax.ppermute(value, axis, [(source, source + steps) for source in range(first, last)])


def passed_along_2(block, axis, distance):
    devices = range(lax.axis_size(axis))
    route = [((i - distance) % len(devices), i) for i in devices]
    return lax.ppermute(block, axis, route)


def normalize(gain_row, shift_row):

    def normalize_mapped(values):
        center = jnp.mean(values, axis=-1, keepdims=True)
        centered = values - center
        spread = jnp.mean(centered * centered, axis=-1, keepdims=True)
        return centered * lax.rsqrt(spread + EPSILON) * gain_row + shift_row

    return normalize_mapped


def gated_gelu(gate_row):

    def gated_mapped(values):
        return gate_row * jax.nn.gelu(values, approximate=False)

    return gated_mapped


def layer_forward(rows_in, tangent_in, gain_row, shift_row, gate_row, weight_mat):
    base_rows = rows_in.astype(jnp.float32)
    tangent_rows = tangent_in.astype(jnp.float32)
    normed, normed_t = jax.jvp(normalize(gain_row, shift_row), (base_rows,), (tangent_rows,))
    normed_pair = jnp.concatenate([normed, normed_t], axis=0).astype(jnp.bfloat16)
    products = jnp.dot(normed_pair, weight_mat, preferred_element_type=jnp.float32)
    row_total = rows_in.shape[0]
    branch, branch_t = jax.jvp(
        gated_gelu(gate_row), (products[:row_total],), (products[row_total:],)
    )
    return (base_rows + branch, tangent_rows + branch_t, normed_pair, products)


def layer_backward(
    rows_in, tangent_in, cotangent, cotangent_t, gain_row, shift_row, gate_row, weight_mat, products
):
    row_total = rows_in.shape[0]

    def branch_pair(values, values_t):
        return jax.jvp(gated_gelu(gate_row), (values,), (values_t,))

    _, pull_back = jax.vjp(branch_pair, products[:row_total], products[row_total:])
    grad_z, grad_zt = pull_back((cotangent, cotangent_t))
    grad_pair = jnp.concatenate([grad_z, grad_zt], axis=0).astype(jnp.bfloat16)
    grad_normed = lax.dot_general(
        grad_pair, weight_mat, (((1,), (1,)), ((), ())), preferred_element_type=jnp.float32
    )

    def norm_pair(values, values_t):
        return jax.jvp(normalize(gain_row, shift_row), (values,), (values_t,))

    _, pull_norm = jax.vjp(norm_pair, rows_in.astype(jnp.float32), tangent_in.astype(jnp.float32))
    grad_rows, grad_tangent = pull_norm((grad_normed[:row_total], grad_normed[row_total:]))
    return (cotangent + grad_rows, cotangent_t + grad_tangent, grad_pair)


def take_slot(stack, position):
    return lax.dynamic_index_in_dim(stack, position, 0, keepdims=False)


def put_slot(stack, value, position):
    return lax.dynamic_update_index_in_dim(stack, value, position, 0)


def body(
    state,
    adjoint,
    probe,
    logp,
    density_weight,
    step_size,
    norm_gain,
    norm_shift,
    branch_gate,
    weights,
):
    sections = lax.axis_size("section")
    section_index = lax.axis_index("section")
    micro_count, row_count, feature_count = state.shape
    gain_row = norm_gain[0]
    shift_row = norm_shift[0]
    gate_row = branch_gate[0]
    weight_mat = weights[0]
    total_steps = micro_count + sections - 1
    at_first = section_index == 0
    at_last = section_index == sections - 1
    blank_rows = jnp.zeros((row_count, feature_count), jnp.bfloat16)
    blank_stack = jnp.zeros((micro_count, row_count, feature_count), jnp.bfloat16)
    pair_blank = jnp.zeros((micro_count, 2 * row_count, feature_count), jnp.bfloat16)
    extras = ()

    def recall(base_rows, base_tangent):
        _, _, normed_pair, products = layer_forward(
            base_rows, base_tangent, gain_row, shift_row, gate_row, weight_mat
        )
        return (normed_pair, products)

    memory = (blank_stack, blank_stack, blank_stack, blank_stack, extras)

    def forward_step(step_number, carried):
        received, memory = carried
        micro_index = step_number - section_index
        active = (micro_index >= 0) & (micro_index < micro_count)
        position = jnp.clip(micro_index, 0, micro_count - 1)
        in_rows = jnp.where(at_first, take_slot(state, position), received[0])
        in_tangent = jnp.where(
            at_first, take_slot(probe, position).astype(jnp.bfloat16), received[1]
        )

        def forward_work_step(memory):
            out_rows, out_tangent, normed_pair, products = layer_forward(
                in_rows, in_tangent, gain_row, shift_row, gate_row, weight_mat
            )
            out_rows = out_rows.astype(jnp.bfloat16)
            out_tangent = out_tangent.astype(jnp.bfloat16)
            top_rows, top_tangent, input_rows, input_tangent, extras = memory
            memory = (
                put_slot(top_rows, out_rows, position),
                put_slot(top_tangent, out_tangent, position),
                put_slot(input_rows, in_rows, position),
                put_slot(input_tangent, in_tangent, position),
                extras,
            )
            return (jnp.stack([out_rows, out_tangent]), memory)

        def forward_skip_step(memory):
            return (jnp.stack([blank_rows, blank_rows]), memory)

        outgoing, memory = lax.cond(active, forward_work_step, forward_skip_step, memory)
        received = passed_along(outgoing, "section", 1)
        return (received, memory)

    start_forward = jnp.zeros((2, row_count, feature_count), jnp.bfloat16)
    _, memory = lax.fori_loop(0, total_steps, forward_step, (start_forward, memory))
    top_rows, top_tangent, input_rows, input_tangent, extras = memory
    slot_total = 5

    def backward_step(step_number, carried):
        received, pair_store, grad_store, own_rows, own_tangent, back_store = carried
        micro_index = step_number - (sections - 1 - section_index)
        active = (micro_index >= 0) & (micro_index < micro_count)
        position = jnp.clip(micro_index, 0, micro_count - 1)

        def backward_work_step(stores):
            pair_store, grad_store, own_rows, own_tangent = stores
            seed_rows = take_slot(adjoint, position).astype(jnp.float32)
            seed_tangent = -take_slot(density_weight, position) * take_slot(probe, position).astype(
                jnp.float32
            )
            cotangent = jnp.where(at_last, seed_rows, received[0].astype(jnp.float32))
            cotangent_t = jnp.where(at_last, seed_tangent, received[1].astype(jnp.float32))
            carry_rows = jnp.where(at_last, take_slot(top_rows, position), received[2])
            carry_tangent = jnp.where(at_last, take_slot(top_tangent, position), received[3])
            base_rows = take_slot(input_rows, position)
            base_tangent = take_slot(input_tangent, position)
            normed_pair, products = recall(base_rows, base_tangent)
            back_rows, back_tangent, grad_pair = layer_backward(
                base_rows,
                base_tangent,
                cotangent,
                cotangent_t,
                gain_row,
                shift_row,
                gate_row,
                weight_mat,
                products,
            )
            mine = micro_index == section_index
            own_rows = jnp.where(mine, carry_rows, own_rows)
            own_tangent = jnp.where(mine, carry_tangent, own_tangent)
            outgoing = jnp.stack(
                [
                    back_rows.astype(jnp.bfloat16),
                    back_tangent.astype(jnp.bfloat16),
                    carry_rows,
                    carry_tangent,
                ]
            )
            return (
                outgoing,
                (
                    put_slot(pair_store, normed_pair, position),
                    put_slot(grad_store, grad_pair, position),
                    own_rows,
                    own_tangent,
                ),
            )

        def backward_skip_step(stores):
            return (jnp.zeros((4, row_count, feature_count), jnp.bfloat16), stores)

        outgoing, stores = lax.cond(
            active,
            backward_work_step,
            backward_skip_step,
            (pair_store, grad_store, own_rows, own_tangent),
        )
        delivered = jnp.where(at_first & active, outgoing[0], received[4])
        received = passed_along_2(
            jnp.concatenate([outgoing, delivered[None]], axis=0), "section", -1
        )
        return (received,) + stores + (back_store,)

    start_backward = jnp.zeros((slot_total, row_count, feature_count), jnp.bfloat16)
    received, pair_store, grad_store, own_rows, own_tangent, back_store = lax.fori_loop(
        0,
        total_steps,
        backward_step,
        (start_backward, pair_blank, pair_blank, blank_rows, blank_rows, blank_stack),
    )
    own_back = received[4]
    step_value = step_size[0]
    own_input = take_slot(state, section_index).astype(jnp.float32)
    state_next = own_input - step_value * (own_rows.astype(jnp.float32) - own_input)
    sign_rows = take_slot(probe, section_index).astype(jnp.float32)
    divergence = jnp.sum(sign_rows * (own_tangent.astype(jnp.float32) - sign_rows)) / (
        row_count * feature_count
    )
    logp_next = (
        lax.dynamic_index_in_dim(logp, section_index, 0, keepdims=True) + step_value * divergence
    )
    own_adjoint = take_slot(adjoint, section_index).astype(jnp.float32)
    adjoint_next = own_adjoint + step_value * (own_back.astype(jnp.float32) - own_adjoint)
    left_rows = pair_store.reshape(micro_count * 2 * row_count, feature_count)
    right_rows = grad_store.reshape(micro_count * 2 * row_count, feature_count)
    grad_share = lax.psum_scatter(
        lax.dot_general(
            left_rows, right_rows, (((0,), (0,)), ((), ())), preferred_element_type=jnp.float32
        ).astype(jnp.bfloat16),
        "dp",
        scatter_dimension=0,
        tiled=True,
    ).astype(jnp.float32)
    return (state_next[None], adjoint_next[None], logp_next, grad_share[None])


def solution(mesh):
    placed = (
        P(None, "dp", None),
        P(None, "dp", None),
        P(None, "dp", None),
        P(None, "dp"),
        P(None, "dp"),
        P(),
        P("section", None),
        P("section", None),
        P("section", None),
        P("section", None, None),
    )
    return jax.shard_map(
        body,
        mesh=mesh,
        in_specs=placed,
        out_specs=(
            P("section", "dp", None),
            P("section", "dp", None),
            P("section", "dp"),
            P("section", "dp", None),
        ),
        check_vma=False,
    )
```

profile of v0, /device:TPU:1, one launch (start us, length us, event | category | flops | bytes accessed | tf_op | source)
XLA Modules:
  0.0 1164.2 jit_solution(17185360232426128286)
XLA Ops:
  9.4 255.4 %while.43 = (s32[]{:T(128)}, bf16[2,16,3072]{2,1,0:T(8,128)(2,1)S(1)}, bf16[8,16,3072]{2,1,0:T(8,128)(2,1)}, bf16[8,16,3072]{2,1,0:T(8,128)(2,1)}, bf16[8,16,307...) while((s32[]{:T(128)}, ...), condition=%wide.region_7.8_spmd, body=%wide.region_0.7_spmd.sunk | while | flops 609878080 | bytes 23938624 | solution.py:153
  9.4 11.5 conditional.4
  11.1 8.0 fusion.21
  25.2 11.5 conditional.4
  26.9 8.0 fusion.21
  43.4 11.5 conditional.4
  61.3 11.5 conditional.4
  79.2 11.5 conditional.4
  80.8 8.0 fusion.21
  97.1 11.4 conditional.4
  114.9 11.5 conditional.4
  132.8 11.4 conditional.4
  150.7 16.7 %collective-permute-start = (bf16[2,16,3072]{2,1,0:T(8,128)(2,1)S(1)}, bf16[2,16,3072]{2,1,0:T(8,128)(2,1)S(1)}, u32[]{:S(2)}, u32[]{:S(2)}) collective-permute-start(bf16[2,16,3072]{2,1,0:T(8,128)(2,1)S(1)} %get-tuple-element.1280), channel_id=1, source_target_pairs={{0,16},{16,32},{32,48},{48,64},{64,80},{80,96},{96,112},{1,17},{17... | collective-permute-start | bytes 589832 | tf_op jit(solution)/shard_map/while/body/eval_jaxpr/ppermute | solution.py:12
  181.3 17.8 %collective-permute-start = (bf16[2,16,3072]{2,1,0:T(8,128)(2,1)S(1)}, bf16[2,16,3072]{2,1,0:T(8,128)(2,1)S(1)}, u32[]{:S(2)}, u32[]{:S(2)}) collective-permute-start(bf16[2,16,3072]{2,1,0:T(8,128)(2,1)S(1)} %get-tuple-element.1280), channel_id=1, source_target_pairs={{0,16},{16,32},{32,48},{48,64},{64,80},{80,96},{96,112},{1,17},{17... | collective-permute-start | bytes 589832 | tf_op jit(solution)/shard_map/while/body/eval_jaxpr/ppermute | solution.py:12
  201.7 9.4 collective-permute-start
  214.7 15.9 %collective-permute-start = (bf16[2,16,3072]{2,1,0:T(8,128)(2,1)S(1)}, bf16[2,16,3072]{2,1,0:T(8,128)(2,1)S(1)}, u32[]{:S(2)}, u32[]{:S(2)}) collective-permute-start(bf16[2,16,3072]{2,1,0:T(8,128)(2,1)S(1)} %get-tuple-element.1280), channel_id=1, source_target_pairs={{0,16},{16,32},{32,48},{48,64},{64,80},{80,96},{96,112},{1,17},{17... | collective-permute-start | bytes 589832 | tf_op jit(solution)/shard_map/while/body/eval_jaxpr/ppermute | solution.py:12
  243.7 18.5 %collective-permute-start = (bf16[2,16,3072]{2,1,0:T(8,128)(2,1)S(1)}, bf16[2,16,3072]{2,1,0:T(8,128)(2,1)S(1)}, u32[]{:S(2)}, u32[]{:S(2)}) collective-permute-start(bf16[2,16,3072]{2,1,0:T(8,128)(2,1)S(1)} %get-tuple-element.1280), channel_id=1, source_target_pairs={{0,16},{16,32},{32,48},{48,64},{64,80},{80,96},{96,112},{1,17},{17... | collective-permute-start | bytes 589832 | tf_op jit(solution)/shard_map/while/body/eval_jaxpr/ppermute | solution.py:12
  267.5 637.6 %while.44 = (s32[]{:T(128)}, bf16[5,16,3072]{2,1,0:T(8,128)(2,1)S(1)}, bf16[8,32,3072]{2,1,0:T(8,128)(2,1)}, bf16[8,32,3072]{2,1,0:T(8,128)(2,1)}, bf16[16,3072]...) while((s32[]{:T(128)}, ...), condition=%wide.region_20.21_spmd, body=%wide.region_8.20_spmd.sunk | while | flops 1220886784 | bytes 50544700 | solution.py:224
  268.3 67.1 %collective-permute-start.1 = (bf16[5,16,3072]{2,1,0:T(8,128)(2,1)S(1)}, bf16[5,16,3072]{2,1,0:T(8,128)(2,1)S(1)}, u32[]{:S(2)}, u32[]{:S(2)}) collective-permute-start(bf16[5,16,3072]{2,1,0:T(8,128)(2,1)S(1)} %pad_maximum_fusion.4), channel_id=1, source_target_pairs={{16,0},{32,16},{48,32},{64,48},{80,64},{96,80},{112,96},{0,112},{1... | collective-permute-start | bytes 1474568 | tf_op jit(solution)/shard_map/while/body/eval_jaxpr/ppermute | solution.py:18
  342.0 35.1 %collective-permute-start.1 = (bf16[5,16,3072]{2,1,0:T(8,128)(2,1)S(1)}, bf16[5,16,3072]{2,1,0:T(8,128)(2,1)S(1)}, u32[]{:S(2)}, u32[]{:S(2)}) collective-permute-start(bf16[5,16,3072]{2,1,0:T(8,128)(2,1)S(1)} %pad_maximum_fusion.4), channel_id=1, source_target_pairs={{16,0},{32,16},{48,32},{64,48},{80,64},{96,80},{112,96},{0,112},{1... | collective-permute-start | bytes 1474568 | tf_op jit(solution)/shard_map/while/body/eval_jaxpr/ppermute | solution.py:18
  383.6 35.1 %collective-permute-start.1 = (bf16[5,16,3072]{2,1,0:T(8,128)(2,1)S(1)}, bf16[5,16,3072]{2,1,0:T(8,128)(2,1)S(1)}, u32[]{:S(2)}, u32[]{:S(2)}) collective-permute-start(bf16[5,16,3072]{2,1,0:T(8,128)(2,1)S(1)} %pad_maximum_fusion.4), channel_id=1, source_target_pairs={{16,0},{32,16},{48,32},{64,48},{80,64},{96,80},{112,96},{0,112},{1... | collective-permute-start | bytes 1474568 | tf_op jit(solution)/shard_map/while/body/eval_jaxpr/ppermute | solution.py:18
  425.2 35.1 %collective-permute-start.1 = (bf16[5,16,3072]{2,1,0:T(8,128)(2,1)S(1)}, bf16[5,16,3072]{2,1,0:T(8,128)(2,1)S(1)}, u32[]{:S(2)}, u32[]{:S(2)}) collective-permute-start(bf16[5,16,3072]{2,1,0:T(8,128)(2,1)S(1)} %pad_maximum_fusion.4), channel_id=1, source_target_pairs={{16,0},{32,16},{48,32},{64,48},{80,64},{96,80},{112,96},{0,112},{1... | collective-permute-start | bytes 1474568 | tf_op jit(solution)/shard_map/while/body/eval_jaxpr/ppermute | solution.py:18
  466.9 35.1 %collective-permute-start.1 = (bf16[5,16,3072]{2,1,0:T(8,128)(2,1)S(1)}, bf16[5,16,3072]{2,1,0:T(8,128)(2,1)S(1)}, u32[]{:S(2)}, u32[]{:S(2)}) collective-permute-start(bf16[5,16,3072]{2,1,0:T(8,128)(2,1)S(1)} %pad_maximum_fusion.4), channel_id=1, source_target_pairs={{16,0},{32,16},{48,32},{64,48},{80,64},{96,80},{112,96},{0,112},{1... | collective-permute-start | bytes 1474568 | tf_op jit(solution)/shard_map/while/body/eval_jaxpr/ppermute | solution.py:18
  508.5 35.1 %collective-permute-start.1 = (bf16[5,16,3072]{2,1,0:T(8,128)(2,1)S(1)}, bf16[5,16,3072]{2,1,0:T(8,128)(2,1)S(1)}, u32[]{:S(2)}, u32[]{:S(2)}) collective-permute-start(bf16[5,16,3072]{2,1,0:T(8,128)(2,1)S(1)} %pad_maximum_fusion.4), channel_id=1, source_target_pairs={{16,0},{32,16},{48,32},{64,48},{80,64},{96,80},{112,96},{0,112},{1... | collective-permute-start | bytes 1474568 | tf_op jit(solution)/shard_map/while/body/eval_jaxpr/ppermute | solution.py:18
  550.2 35.1 %collective-permute-start.1 = (bf16[5,16,3072]{2,1,0:T(8,128)(2,1)S(1)}, bf16[5,16,3072]{2,1,0:T(8,128)(2,1)S(1)}, u32[]{:S(2)}, u32[]{:S(2)}) collective-permute-start(bf16[5,16,3072]{2,1,0:T(8,128)(2,1)S(1)} %pad_maximum_fusion.4), channel_id=1, source_target_pairs={{16,0},{32,16},{48,32},{64,48},{80,64},{96,80},{112,96},{0,112},{1... | collective-permute-start | bytes 1474568 | tf_op jit(solution)/shard_map/while/body/eval_jaxpr/ppermute | solution.py:18
  591.0 30.2 %conditional.5 = (bf16[4,16,3072]{2,1,0:T(8,128)(2,1)S(1)}, bf16[8,32,3072]{2,1,0:T(8,128)(2,1)}, bf16[8,32,3072]{2,1,0:T(8,128)(2,1)}, bf16[16,3072]{1,0:T(8,12...) conditional(s32[]{:T(128)} %convert_element_type.381, (bf16[8,32,3072]{2,1,0:T(8,128)(2,1)}, ...), branch_computations={%region_9.9_spmd, %region_10.19_spmd} | conditional | flops 1220591872 | bytes 47300192 | solution.py:211
  593.4 8.0 fusion.70
  605.4 9.4 fusion.74
  632.7 30.2 %conditional.5 = (bf16[4,16,3072]{2,1,0:T(8,128)(2,1)S(1)}, bf16[8,32,3072]{2,1,0:T(8,128)(2,1)}, bf16[8,32,3072]{2,1,0:T(8,128)(2,1)}, bf16[16,3072]{1,0:T(8,12...) conditional(s32[]{:T(128)} %convert_element_type.381, (bf16[8,32,3072]{2,1,0:T(8,128)(2,1)}, ...), branch_computations={%region_9.9_spmd, %region_10.19_spmd} | conditional | flops 1220591872 | bytes 47300192 | solution.py:211
  647.0 9.4 fusion.74
  671.6 30.2 %conditional.5 = (bf16[4,16,3072]{2,1,0:T(8,128)(2,1)S(1)}, bf16[8,32,3072]{2,1,0:T(8,128)(2,1)}, bf16[8,32,3072]{2,1,0:T(8,128)(2,1)}, bf16[16,3072]{1,0:T(8,12...) conditional(s32[]{:T(128)} %convert_element_type.381, (bf16[8,32,3072]{2,1,0:T(8,128)(2,1)}, ...), branch_computations={%region_9.9_spmd, %region_10.19_spmd} | conditional | flops 1220591872 | bytes 47300192 | solution.py:211
  685.9 9.4 fusion.74
  710.5 30.2 %conditional.5 = (bf16[4,16,3072]{2,1,0:T(8,128)(2,1)S(1)}, bf16[8,32,3072]{2,1,0:T(8,128)(2,1)}, bf16[8,32,3072]{2,1,0:T(8,128)(2,1)}, bf16[16,3072]{1,0:T(8,12...) conditional(s32[]{:T(128)} %convert_element_type.381, (bf16[8,32,3072]{2,1,0:T(8,128)(2,1)}, ...), branch_computations={%region_9.9_spmd, %region_10.19_spmd} | conditional | flops 1220591872 | bytes 47300192 | solution.py:211
  712.8 8.0 fusion.70
  724.8 9.4 fusion.74
  749.4 30.2 %conditional.5 = (bf16[4,16,3072]{2,1,0:T(8,128)(2,1)S(1)}, bf16[8,32,3072]{2,1,0:T(8,128)(2,1)}, bf16[8,32,3072]{2,1,0:T(8,128)(2,1)}, bf16[16,3072]{1,0:T(8,12...) conditional(s32[]{:T(128)} %convert_element_type.381, (bf16[8,32,3072]{2,1,0:T(8,128)(2,1)}, ...), branch_computations={%region_9.9_spmd, %region_10.19_spmd} | conditional | flops 1220591872 | bytes 47300192 | solution.py:211
  751.8 8.0 fusion.70
  763.8 9.4 fusion.74
  788.4 30.2 %conditional.5 = (bf16[4,16,3072]{2,1,0:T(8,128)(2,1)S(1)}, bf16[8,32,3072]{2,1,0:T(8,128)(2,1)}, bf16[8,32,3072]{2,1,0:T(8,128)(2,1)}, bf16[16,3072]{1,0:T(8,12...) conditional(s32[]{:T(128)} %convert_element_type.381, (bf16[8,32,3072]{2,1,0:T(8,128)(2,1)}, ...), branch_computations={%region_9.9_spmd, %region_10.19_spmd} | conditional | flops 1220591872 | bytes 47300192 | solution.py:211
  790.7 8.0 fusion.70
  802.7 9.4 fusion.74
  827.3 30.2 %conditional.5 = (bf16[4,16,3072]{2,1,0:T(8,128)(2,1)S(1)}, bf16[8,32,3072]{2,1,0:T(8,128)(2,1)}, bf16[8,32,3072]{2,1,0:T(8,128)(2,1)}, bf16[16,3072]{1,0:T(8,12...) conditional(s32[]{:T(128)} %convert_element_type.381, (bf16[8,32,3072]{2,1,0:T(8,128)(2,1)}, ...), branch_computations={%region_9.9_spmd, %region_10.19_spmd} | conditional | flops 1220591872 | bytes 47300192 | solution.py:211
  829.6 8.0 fusion.70
  841.6 9.4 fusion.74
  866.2 30.2 %conditional.5 = (bf16[4,16,3072]{2,1,0:T(8,128)(2,1)S(1)}, bf16[8,32,3072]{2,1,0:T(8,128)(2,1)}, bf16[8,32,3072]{2,1,0:T(8,128)(2,1)}, bf16[16,3072]{1,0:T(8,12...) conditional(s32[]{:T(128)} %convert_element_type.381, (bf16[8,32,3072]{2,1,0:T(8,128)(2,1)}, ...), branch_computations={%region_9.9_spmd, %region_10.19_spmd} | conditional | flops 1220591872 | bytes 47300192 | solution.py:211
  880.5 9.4 fusion.74
  905.1 10.9 bitcast_convert_fusion
  923.4 229.9 %reduce-scatter.2.cloned.1.call-done = bf16[192,3072]{1,0:T(8,128)(2,1)} async-done(((bf16[3072,3072]{1,0:T(8,128)(2,1)}), bf16[192,3072]{1,0:T(8,128)(2,1)}) %reduce-scatter.2.cloned.1.call-update) | async-done | bytes 1179664 | tf_op jit(solution)/shard_map/reduce_scatter | solution.py:245
  (404 shorter events, 414.4 us)
Async XLA Ops:
  7.2 909.6 %copy-start = (f32[8,1]{0,1:T(1,128)S(1)}, f32[8,1]{0,1:T(1,128)}, u32[]{:S(2)}) copy-start(f32[8,1]{0,1:T(1,128)} %param.21) | copy-start | bytes 100
  7.2 1146.2 %reduce-scatter.2.cloned.1.call-start = ((), (), s32[]{:S(2)}) async-start(), calls=%async_computation.1 | async-start | bytes 20054016 | tf_op jit(solution)/shard_map/reduce_scatter | solution.py:245
  7.3 2.1 copy-start.1
  7.3 2.1 copy-start.2
  7.3 2.1 copy-start.3
  20.9 4.3 collective-permute-start
  36.7 6.7 collective-permute-start
  54.9 6.4 collective-permute-start
  72.8 6.4 collective-permute-start
  90.6 6.4 collective-permute-start
  108.5 6.4 collective-permute-start
  126.4 6.4 collective-permute-start
  144.3 6.4 collective-permute-start
  150.7 19.3 %collective-permute-start = (bf16[2,16,3072]{2,1,0:T(8,128)(2,1)S(1)}, bf16[2,16,3072]{2,1,0:T(8,128)(2,1)S(1)}, u32[]{:S(2)}, u32[]{:S(2)}) collective-permute-start(bf16[2,16,3072]{2,1,0:T(8,128)(2,1)S(1)} %get-tuple-element.1280), channel_id=1, source_target_pairs={{0,16},{16,32},{32,48},{48,64},{64,80},{80,96},{96,112},{1,17},{17... | collective-permute-start | bytes 589832 | tf_op jit(solution)/shard_map/while/body/eval_jaxpr/ppermute | solution.py:12
  170.1 11.1 collective-permute-start
  181.3 20.4 %collective-permute-start = (bf16[2,16,3072]{2,1,0:T(8,128)(2,1)S(1)}, bf16[2,16,3072]{2,1,0:T(8,128)(2,1)S(1)}, u32[]{:S(2)}, u32[]{:S(2)}) collective-permute-start(bf16[2,16,3072]{2,1,0:T(8,128)(2,1)S(1)} %get-tuple-element.1280), channel_id=1, source_target_pairs={{0,16},{16,32},{32,48},{48,64},{64,80},{80,96},{96,112},{1,17},{17... | collective-permute-start | bytes 589832 | tf_op jit(solution)/shard_map/while/body/eval_jaxpr/ppermute | solution.py:12
  201.7 13.0 %collective-permute-start = (bf16[2,16,3072]{2,1,0:T(8,128)(2,1)S(1)}, bf16[2,16,3072]{2,1,0:T(8,128)(2,1)S(1)}, u32[]{:S(2)}, u32[]{:S(2)}) collective-permute-start(bf16[2,16,3072]{2,1,0:T(8,128)(2,1)S(1)} %get-tuple-element.1280), channel_id=1, source_target_pairs={{0,16},{16,32},{32,48},{48,64},{64,80},{80,96},{96,112},{1,17},{17... | collective-permute-start | bytes 589832 | tf_op jit(solution)/shard_map/while/body/eval_jaxpr/ppermute | solution.py:12
  214.7 18.5 %collective-permute-start = (bf16[2,16,3072]{2,1,0:T(8,128)(2,1)S(1)}, bf16[2,16,3072]{2,1,0:T(8,128)(2,1)S(1)}, u32[]{:S(2)}, u32[]{:S(2)}) collective-permute-start(bf16[2,16,3072]{2,1,0:T(8,128)(2,1)S(1)} %get-tuple-element.1280), channel_id=1, source_target_pairs={{0,16},{16,32},{32,48},{48,64},{64,80},{80,96},{96,112},{1,17},{17... | collective-permute-start | bytes 589832 | tf_op jit(solution)/shard_map/while/body/eval_jaxpr/ppermute | solution.py:12
  233.2 10.4 collective-permute-start
  243.7 21.1 %collective-permute-start = (bf16[2,16,3072]{2,1,0:T(8,128)(2,1)S(1)}, bf16[2,16,3072]{2,1,0:T(8,128)(2,1)S(1)}, u32[]{:S(2)}, u32[]{:S(2)}) collective-permute-start(bf16[2,16,3072]{2,1,0:T(8,128)(2,1)S(1)} %get-tuple-element.1280), channel_id=1, source_target_pairs={{0,16},{16,32},{32,48},{48,64},{64,80},{80,96},{96,112},{1,17},{17... | collective-permute-start | bytes 589832 | tf_op jit(solution)/shard_map/while/body/eval_jaxpr/ppermute | solution.py:12
  264.8 2.7 copy-start.4
  268.3 72.9 %collective-permute-start.1 = (bf16[5,16,3072]{2,1,0:T(8,128)(2,1)S(1)}, bf16[5,16,3072]{2,1,0:T(8,128)(2,1)S(1)}, u32[]{:S(2)}, u32[]{:S(2)}) collective-permute-start(bf16[5,16,3072]{2,1,0:T(8,128)(2,1)S(1)} %pad_maximum_fusion.4), channel_id=1, source_target_pairs={{16,0},{32,16},{48,32},{64,48},{80,64},{96,80},{112,96},{0,112},{1... | collective-permute-start | bytes 1474568 | tf_op jit(solution)/shard_map/while/body/eval_jaxpr/ppermute | solution.py:18
  342.0 40.8 %collective-permute-start.1 = (bf16[5,16,3072]{2,1,0:T(8,128)(2,1)S(1)}, bf16[5,16,3072]{2,1,0:T(8,128)(2,1)S(1)}, u32[]{:S(2)}, u32[]{:S(2)}) collective-permute-start(bf16[5,16,3072]{2,1,0:T(8,128)(2,1)S(1)} %pad_maximum_fusion.4), channel_id=1, source_target_pairs={{16,0},{32,16},{48,32},{64,48},{80,64},{96,80},{112,96},{0,112},{1... | collective-permute-start | bytes 1474568 | tf_op jit(solution)/shard_map/while/body/eval_jaxpr/ppermute | solution.py:18
  383.6 40.8 %collective-permute-start.1 = (bf16[5,16,3072]{2,1,0:T(8,128)(2,1)S(1)}, bf16[5,16,3072]{2,1,0:T(8,128)(2,1)S(1)}, u32[]{:S(2)}, u32[]{:S(2)}) collective-permute-start(bf16[5,16,3072]{2,1,0:T(8,128)(2,1)S(1)} %pad_maximum_fusion.4), channel_id=1, source_target_pairs={{16,0},{32,16},{48,32},{64,48},{80,64},{96,80},{112,96},{0,112},{1... | collective-permute-start | bytes 1474568 | tf_op jit(solution)/shard_map/while/body/eval_jaxpr/ppermute | solution.py:18
  425.2 40.9 %collective-permute-start.1 = (bf16[5,16,3072]{2,1,0:T(8,128)(2,1)S(1)}, bf16[5,16,3072]{2,1,0:T(8,128)(2,1)S(1)}, u32[]{:S(2)}, u32[]{:S(2)}) collective-permute-start(bf16[5,16,3072]{2,1,0:T(8,128)(2,1)S(1)} %pad_maximum_fusion.4), channel_id=1, source_target_pairs={{16,0},{32,16},{48,32},{64,48},{80,64},{96,80},{112,96},{0,112},{1... | collective-permute-start | bytes 1474568 | tf_op jit(solution)/shard_map/while/body/eval_jaxpr/ppermute | solution.py:18
  466.9 40.9 %collective-permute-start.1 = (bf16[5,16,3072]{2,1,0:T(8,128)(2,1)S(1)}, bf16[5,16,3072]{2,1,0:T(8,128)(2,1)S(1)}, u32[]{:S(2)}, u32[]{:S(2)}) collective-permute-start(bf16[5,16,3072]{2,1,0:T(8,128)(2,1)S(1)} %pad_maximum_fusion.4), channel_id=1, source_target_pairs={{16,0},{32,16},{48,32},{64,48},{80,64},{96,80},{112,96},{0,112},{1... | collective-permute-start | bytes 1474568 | tf_op jit(solution)/shard_map/while/body/eval_jaxpr/ppermute | solution.py:18
  508.5 40.9 %collective-permute-start.1 = (bf16[5,16,3072]{2,1,0:T(8,128)(2,1)S(1)}, bf16[5,16,3072]{2,1,0:T(8,128)(2,1)S(1)}, u32[]{:S(2)}, u32[]{:S(2)}) collective-permute-start(bf16[5,16,3072]{2,1,0:T(8,128)(2,1)S(1)} %pad_maximum_fusion.4), channel_id=1, source_target_pairs={{16,0},{32,16},{48,32},{64,48},{80,64},{96,80},{112,96},{0,112},{1... | collective-permute-start | bytes 1474568 | tf_op jit(solution)/shard_map/while/body/eval_jaxpr/ppermute | solution.py:18
  550.2 40.8 %collective-permute-start.1 = (bf16[5,16,3072]{2,1,0:T(8,128)(2,1)S(1)}, bf16[5,16,3072]{2,1,0:T(8,128)(2,1)S(1)}, u32[]{:S(2)}, u32[]{:S(2)}) collective-permute-start(bf16[5,16,3072]{2,1,0:T(8,128)(2,1)S(1)} %pad_maximum_fusion.4), channel_id=1, source_target_pairs={{16,0},{32,16},{48,32},{64,48},{80,64},{96,80},{112,96},{0,112},{1... | collective-permute-start | bytes 1474568 | tf_op jit(solution)/shard_map/while/body/eval_jaxpr/ppermute | solution.py:18
  622.2 10.5 collective-permute-start.1
  663.8 7.7 collective-permute-start.1
  702.8 7.7 collective-permute-start.1
  741.7 7.7 collective-permute-start.1
  780.6 7.7 collective-permute-start.1
  819.5 7.7 collective-permute-start.1
  858.5 7.7 collective-permute-start.1
  897.4 7.7 collective-permute-start.1
Sparse Core Ops, SparseCore 0:
  916.2 237.0 reduce-scatter.1
where the time goes:
time: 1170 us; the launch traced here: 1160 us
  starting transfers between devices  405 us (35%)
  waiting for transfers between devices  371 us (32%)
  matrix products  215 us (18%)
  other arithmetic  145 us (12%)
  between operations  17.2 us (1%)
    ppermute x15, starting transfers between devices, passed_along_2(): return lax.ppermute(block, axis, route)  283 us
    reduce_scatter x1, waiting for transfers between devices, body(): lax.psum_scatter(lax.dot_general(left_rows, right_rows, (((0,), (0,)), ((...  230 us
    dot_general x16, matrix products, layer_forward(): jnp.dot(normed_pair, weight_mat, preferred_element_type=jnp.float32)  128 us
    ppermute x15, starting transfers between devices, passed_along(): lax.ppermute(value, axis, [(source, source + steps) for source in range(f...  122 us
    ppermute x15, waiting for transfers between devices, passed_along_2(): return lax.ppermute(block, axis, route)  99.8 us
    dot_general x8, matrix products, layer_backward(): lax.dot_general(grad_pair, weight_mat, (((1,), (1,)), ((), ())), preferre...  75.6 us
    ppermute x15, waiting for transfers between devices, passed_along(): lax.ppermute(value, axis, [(source, source + steps) for source in range(f...  41.3 us
    another operation x40, other arithmetic  35.4 us
  transfers between devices with their start and end apart: 31, of which 31 were waited for; matrix products, arithmetic and copies ran while one was open for 0% of the time, Pallas kernels for 0%

commit v1 on v0

v1 whole, which is shorter than its diff:
```python
import functools

import jax
import jax.numpy as jnp
from jax import lax
from jax.experimental import pallas as pl
from jax.experimental.pallas import tpu as pltpu
from jax.sharding import PartitionSpec as P

EPSILON = 1e-06
MESH = pl.DeviceIdType.MESH
CHUNKS = 4
ROOT_HALF = 0.7071067811865476
PHI_SCALE = 0.3989422804014327
F32 = jnp.float32
BF16 = jnp.bfloat16


def wait_bytes(ref, sem):
    pltpu.make_async_copy(ref, ref, sem).wait()


def lanes(value):
    total = value[:, 0:128]
    for at in range(128, value.shape[1], 128):
        total = total + value[:, at : at + 128]
    return total


def kernel(
    sections, dp_size, tok, feat,
    xs_hbm, cs_hbm, dw_hbm, gain_ref, shift_ref, gate_ref, w_hbm,
    fin_u, fin_b, fin_div, grad_out,
    w_vm, wt_vm, x_in, out_buf, c_in, n_buf, n_loc, g_loc, n_all, g_all,
    g1_buf, g2_buf, ab_buf, stats, scale, div_buf, ex_recv,
    w_sem, in_sem, x_ssem, x_rsem, c_ssem, c_rsem, n_ssem, n_rsem, g_ssem, g_rsem,
    fu_rsem, fb_rsem, dv_ssem, dv_rsem, sc_ssem, sc_rsem, e_ssem, e_rsem, f_ssem, f_rsem,
):
    micros = sections
    cw = feat // CHUNKS
    pair = 2 * tok
    chips = dp_size // 2
    halves = chips // 4
    ncols = feat // halves
    keep = ncols // 2
    piece = keep // 4
    tile = 256
    inv = 1.0 / feat
    half_section = sections // 2
    last = sections - 1

    s = lax.axis_index("section")
    d = lax.axis_index("dp")
    core = lax.rem(d, 2)
    chip = lax.div(d, 2)
    x_at = lax.rem(chip, 2)
    d_flip = d + 2 - 4 * x_at
    z_at = lax.div(chip, 2)
    my_half = lax.div(chip, 4)
    my_col = lax.rem(chip, 4)
    next_d = jnp.where(s == half_section - 1, d_flip, d)
    prev_d = jnp.where(s == half_section, d_flip, d)

    def w_copy(k):
        cols = pl.ds(k * cw, cw)
        return pltpu.make_async_copy(w_hbm.at[:, cols], w_vm.at[:, cols], w_sem.at[k])

    for k in range(CHUNKS):
        w_copy(k).start()

    def x_copy(m):
        return pltpu.make_async_copy(xs_hbm.at[m], x_in.at[m], in_sem.at[m])

    @pl.when(s == 0)
    def _():
        for m in range(micros):
            x_copy(m).start()

    barrier = pltpu.get_barrier_semaphore()

    def greet_group(i, carry):
        other = lax.rem(d + i, dp_size)
        pl.semaphore_signal(barrier, inc=1, device_id=(s, other), device_id_type=MESH)
        return carry

    def greet_sections(i, carry):
        other = lax.rem(s + i, sections)
        pl.semaphore_signal(barrier, inc=1, device_id=(other, d), device_id_type=MESH)
        pl.semaphore_signal(barrier, inc=1, device_id=(other, d_flip), device_id_type=MESH)
        return carry

    lax.fori_loop(1, dp_size, greet_group, 0)
    lax.fori_loop(1, sections, greet_sections, 0)
    pl.semaphore_wait(barrier, dp_size - 1 + 2 * (sections - 1))

    def seed_copy(m):
        return pltpu.make_async_remote_copy(
            src_ref=cs_hbm.at[m],
            dst_ref=c_in.at[m],
            send_sem=c_ssem.at[m, 0],
            recv_sem=c_rsem.at[m, 0],
            device_id=(s, d_flip),
            device_id_type=MESH,
        )

    def scale_copy():
        return pltpu.make_async_remote_copy(
            src_ref=dw_hbm,
            dst_ref=scale,
            send_sem=sc_ssem,
            recv_sem=sc_rsem,
            device_id=(s, d_flip),
            device_id_type=MESH,
        )

    @pl.when(s == last)
    def _():
        scale_copy().start()
        for m in range(micros):
            seed_copy(m).start()

    @pl.when(s != last)
    def _():
        scale[...] = jnp.ones_like(scale)

    def transpose_weights():
        count = feat // tile

        def one(i, carry):
            at_row = pl.multiple_of(lax.div(i, count) * tile, tile)
            at_col = pl.multiple_of(lax.rem(i, count) * tile, tile)
            wt_vm[pl.ds(at_col, tile), pl.ds(at_row, tile)] = w_vm[
                pl.ds(at_row, tile), pl.ds(at_col, tile)
            ].T
            return carry

        lax.fori_loop(0, count * count, one, 0)

    @pl.when(s >= half_section)
    def _():
        for k in range(CHUNKS):
            w_copy(k).wait()
        transpose_weights()

    def x_send(m, k):
        return pltpu.make_async_remote_copy(
            src_ref=out_buf.at[m, k],
            dst_ref=x_in.at[m, k],
            send_sem=x_ssem.at[m, k],
            recv_sem=x_rsem.at[m, k],
            device_id=(s + 1, next_d),
            device_id_type=MESH,
        )

    def top_send(m, k):
        return pltpu.make_async_remote_copy(
            src_ref=out_buf.at[m, k, pl.ds(0, tok)],
            dst_ref=fin_u.at[k],
            send_sem=x_ssem.at[m, k],
            recv_sem=fu_rsem.at[k],
            device_id=(m, d_flip),
            device_id_type=MESH,
        )

    def gather_send(loc, everything, ssem, rsem, m, index, other):
        return pltpu.make_async_remote_copy(
            src_ref=loc.at[m, index],
            dst_ref=everything.at[m, chip],
            send_sem=ssem.at[m],
            recv_sem=rsem.at[m],
            device_id=(s, other * 2 + core),
            device_id_type=MESH,
        )

    def forward(m, carry):
        @pl.when(s == 0)
        def _():
            x_copy(m).wait()

        @pl.when(s > 0)
        def _():
            for k in range(CHUNKS):
                wait_bytes(x_in.at[m, k], x_rsem.at[m, k])

        def rows(k):
            return x_in[m, k, pl.ds(0, tok), :].astype(F32)

        def tangents(k):
            return x_in[m, k, pl.ds(tok, tok), :].astype(F32)

        total_u = total_w = 0.0
        for k in range(CHUNKS):
            total_u = total_u + lanes(rows(k))
            total_w = total_w + lanes(tangents(k))
        mean_u = jnp.sum(total_u, axis=1, keepdims=True) * inv
        mean_w = jnp.sum(total_w, axis=1, keepdims=True) * inv
        square = cross = 0.0
        for k in range(CHUNKS):
            centered = rows(k) - mean_u
            square = square + lanes(centered * centered)
            cross = cross + lanes(centered * (tangents(k) - mean_w))
        var = jnp.sum(square, axis=1, keepdims=True) * inv
        cov = jnp.sum(cross, axis=1, keepdims=True) * inv
        rinv = lax.rsqrt(var + EPSILON)
        slope = rinv * cov
        for at, value in enumerate((mean_u, mean_w, rinv, slope)):
            stats[m, at] = jnp.broadcast_to(value, (tok, 128))
        for k in range(CHUNKS):
            cols = pl.ds(k * cw, cw)
            gain = gain_ref[:, cols]
            xhat = (rows(k) - mean_u) * rinv
            normed = xhat * gain + shift_ref[:, cols]
            normed_t = rinv * ((tangents(k) - mean_w) - xhat * slope) * gain
            n_buf[pl.ds(0, tok), cols] = normed.astype(BF16)
            n_buf[pl.ds(tok, tok), cols] = normed_t.astype(BF16)
        for at in range(halves):
            n_loc[m, at] = n_buf[:, pl.ds(at * ncols, ncols)]

        def send_n(i, carry):
            other = lax.rem(chip + i, chips)
            gather_send(n_loc, n_all, n_ssem, n_rsem, m, lax.div(other, 4), other).start()
            return carry

        lax.fori_loop(1, chips, send_n, 0)
        n_all[m, chip] = n_loc[m, my_half]

        for k in range(CHUNKS):
            cols = pl.ds(k * cw, cw)

            @pl.when((m == 0) & (s < half_section))
            def _():
                w_copy(k).wait()

            product = jnp.dot(n_buf[...], w_vm[:, cols], preferred_element_type=F32)
            z = product[:tok]
            z_t = product[tok:]
            gate = gate_ref[:, cols]
            cdf = 0.5 + 0.5 * lax.erf(z * ROOT_HALF)
            zz = z * z
            pdf = PHI_SCALE * jnp.exp(-0.5 * zz)
            first = gate * (cdf + z * pdf)
            out_buf[m, k, pl.ds(0, tok), :] = (rows(k) + gate * (z * cdf)).astype(BF16)
            out_buf[m, k, pl.ds(tok, tok), :] = (tangents(k) + first * z_t).astype(BF16)

            @pl.when(s < last)
            def _():
                x_send(m, k).start()

            @pl.when(s == last)
            def _():
                top_send(m, k).start()

            g1_buf[m, k] = first
            g2_buf[m, k] = gate * (pdf * (2.0 - zz)) * z_t
        return carry

    lax.fori_loop(0, micros, forward, 0)

    @pl.when(s < half_section)
    def _():
        transpose_weights()

    @pl.when(s == last)
    def _():
        wait_bytes(scale, sc_rsem)
        scale_copy().wait_send()
        for m in range(micros):
            seed_copy(m).wait_send()

    def c_send(m, k):
        return pltpu.make_async_remote_copy(
            src_ref=out_buf.at[m, k],
            dst_ref=c_in.at[m, k],
            send_sem=c_ssem.at[m, k],
            recv_sem=c_rsem.at[m, k],
            device_id=(s - 1, prev_d),
            device_id_type=MESH,
        )

    def back_send(m, k):
        return pltpu.make_async_remote_copy(
            src_ref=out_buf.at[m, k, pl.ds(0, tok)],
            dst_ref=fin_b.at[k],
            send_sem=c_ssem.at[m, k],
            recv_sem=fb_rsem.at[k],
            device_id=(m, d),
            device_id_type=MESH,
        )

    def back_own(k):
        return pltpu.make_async_copy(
            out_buf.at[0, k, pl.ds(0, tok)], fin_b.at[k], fb_rsem.at[k]
        )

    def div_send(m):
        return pltpu.make_async_remote_copy(
            src_ref=div_buf.at[m],
            dst_ref=fin_div,
            send_sem=dv_ssem.at[m],
            recv_sem=dv_rsem,
            device_id=(m, d_flip),
            device_id_type=MESH,
        )

    def backward(m, carry):
        @pl.when(s == last)
        def _():
            wait_bytes(c_in.at[m], c_rsem.at[m, 0])
            total = 0.0
            for k in range(CHUNKS):
                sign = c_in[m, k, pl.ds(tok, tok), :].astype(F32)
                top = out_buf[m, k, pl.ds(tok, tok), :].astype(F32)
                total = total + lanes(sign * (top - sign))
            div_buf[m] = total[:8] + total[8:]
            div_send(m).start()
            for k in range(CHUNKS):
                top_send(m, k).wait_send()

        @pl.when(s < last)
        def _():
            for k in range(CHUNKS):
                wait_bytes(c_in.at[m, k], c_rsem.at[m, k])
                x_send(m, k).wait_send()

        factor = scale[m, 0:1, 0:1]

        def cot(k):
            return c_in[m, k, pl.ds(0, tok), :].astype(F32)

        def cot_t(k):
            return c_in[m, k, pl.ds(tok, tok), :].astype(F32) * factor

        for k in range(CHUNKS):
            cols = pl.ds(k * cw, cw)
            first = g1_buf[m, k]
            c_t = cot_t(k)
            top = (cot(k) * first + c_t * g2_buf[m, k]).astype(BF16)
            low = (c_t * first).astype(BF16)
            n_buf[pl.ds(0, tok), cols] = top
            n_buf[pl.ds(tok, tok), cols] = low
            g_loc[m, k, pl.ds(0, tok), :] = top
            g_loc[m, k, pl.ds(tok, tok), :] = low

        def send_g(i, carry):
            other = lax.rem(chip + i, chips)
            gather_send(g_loc, g_all, g_ssem, g_rsem, m, lax.rem(other, 4), other).start()
            return carry

        lax.fori_loop(1, chips, send_g, 0)
        g_all[m, chip] = g_loc[m, my_col]

        mean_u = stats[m, 0][:, 0:1]
        mean_w = stats[m, 1][:, 0:1]
        rinv = stats[m, 2][:, 0:1]
        slope = stats[m, 3][:, 0:1]

        def hat(k):
            return (x_in[m, k, pl.ds(0, tok), :].astype(F32) - mean_u) * rinv

        def centered_w(k):
            return x_in[m, k, pl.ds(tok, tok), :].astype(F32) - mean_w

        sums = [0.0] * 5
        for k in range(CHUNKS):
            cols = pl.ds(k * cw, cw)
            product = jnp.dot(n_buf[...], wt_vm[:, cols], preferred_element_type=F32)
            gain = gain_ref[:, cols]
            a = product[:tok] * gain
            b = product[tok:] * gain
            ab_buf[k, pl.ds(0, tok), :] = a
            ab_buf[k, pl.ds(tok, tok), :] = b
            xhat = hat(k)
            for at, value in enumerate((a, a * xhat, b, b * xhat, b * centered_w(k))):
                sums[at] = sums[at] + lanes(value)
        mean_a, mean_ax, mean_b, mean_bx, mean_bw = (
            jnp.sum(value, axis=1, keepdims=True) * inv for value in sums
        )
        square = rinv * rinv
        for k in range(CHUNKS):
            xhat = hat(k)
            a = ab_buf[k, pl.ds(0, tok), :]
            b = ab_buf[k, pl.ds(tok, tok), :] - mean_b
            back_u = (
                cot(k)
                + rinv * (a - mean_a - xhat * mean_ax)
                - square
                * (
                    xhat * (mean_bw - 3.0 * mean_bx * slope)
                    + slope * b
                    + mean_bx * centered_w(k)
                )
            )
            back_w = cot_t(k) + rinv * (b - xhat * mean_bx)
            out_buf[m, k, pl.ds(0, tok), :] = back_u.astype(BF16)
            out_buf[m, k, pl.ds(tok, tok), :] = back_w.astype(BF16)

            @pl.when(s > 0)
            def _():
                c_send(m, k).start()

            @pl.when((s == 0) & (m > 0))
            def _():
                back_send(m, k).start()

            @pl.when((s == 0) & (m == 0))
            def _():
                back_own(k).start()

        return carry

    lax.fori_loop(0, micros, backward, 0)

    def arrived(m, carry):
        wait_bytes(n_all.at[m, pl.ds(0, chips - 1)], n_rsem.at[m])
        wait_bytes(g_all.at[m, pl.ds(0, chips - 1)], g_rsem.at[m])
        return carry

    lax.fori_loop(0, micros, arrived, 0)

    half_micros = micros // 2
    depth = half_micros * chips * pair
    tiles = keep // tile
    ex_send = w_vm.at[pl.ds(0, keep), pl.ds(0, cw)]
    fin_send = w_vm.at[pl.ds(keep, keep), pl.ds(0, cw)]

    def block(start):
        cols = pl.ds(pl.multiple_of(start, tile), tile)
        total = 0.0
        for first in (0, half_micros):
            some = pl.ds(first, half_micros)
            left = n_all[some, :, :, cols].reshape(depth, tile)
            right = g_all[some].reshape(depth, cw)
            total = total + lax.dot_general(
                left, right, (((0,), (0,)), ((), ())), preferred_element_type=F32
            )
        return total

    def ex_copy(i):
        at = pl.ds(i * tile, tile)
        return pltpu.make_async_remote_copy(
            src_ref=ex_send.at[at],
            dst_ref=ex_recv.at[at],
            send_sem=e_ssem.at[i],
            recv_sem=e_rsem.at[i],
            device_id=(s, d + 1 - 2 * core),
            device_id_type=MESH,
        )

    for i in range(tiles):
        ex_send[pl.ds(i * tile, tile), :] = block((1 - core) * keep + i * tile).astype(BF16)
        ex_copy(i).start()
    for i in range(tiles):
        at = pl.ds(i * tile, tile)
        mine = block(core * keep + i * tile)
        wait_bytes(ex_recv.at[at], e_rsem.at[i])
        fin_send[at, :] = (mine + ex_recv[at, :].astype(F32)).astype(BF16)

    goal = (2 * my_half + core) * 4

    def piece_send(j):
        return pltpu.make_async_remote_copy(
            src_ref=fin_send.at[pl.ds(j * piece, piece)],
            dst_ref=grad_out.at[my_col],
            send_sem=f_ssem.at[j],
            recv_sem=f_rsem.at[my_col],
            device_id=(s, goal + j),
            device_id_type=MESH,
        )

    def piece_own(j):
        return pltpu.make_async_copy(
            fin_send.at[pl.ds(j * piece, piece)], grad_out.at[my_col], f_rsem.at[my_col]
        )

    for j in range(4):

        @pl.when(goal + j != d)
        def _():
            piece_send(j).start()

        @pl.when(goal + j == d)
        def _():
            piece_own(j).start()

    for k in range(CHUNKS):
        wait_bytes(fin_u.at[k], fu_rsem.at[k])
        wait_bytes(fin_b.at[k], fb_rsem.at[k])
    wait_bytes(fin_div, dv_rsem)

    def drain(m, carry):
        wait_bytes(n_all.at[m, pl.ds(0, chips - 1)], n_ssem.at[m])
        wait_bytes(g_all.at[m, pl.ds(0, chips - 1)], g_ssem.at[m])

        @pl.when(s == last)
        def _():
            div_send(m).wait_send()

        @pl.when(s > 0)
        def _():
            for k in range(CHUNKS):
                c_send(m, k).wait_send()

        @pl.when((s == 0) & (m > 0))
        def _():
            for k in range(CHUNKS):
                back_send(m, k).wait_send()

        return carry

    lax.fori_loop(0, micros, drain, 0)
    for i in range(tiles):
        ex_copy(i).wait_send()
    for j in range(4):

        @pl.when(goal + j != d)
        def _():
            piece_send(j).wait_send()

        wait_bytes(grad_out.at[j], f_rsem.at[j])


def run_kernel(sections, dp_size, tok, feat, *operands):
    micros = sections
    cw = feat // CHUNKS
    pair = 2 * tok
    chips = dp_size // 2
    halves = chips // 4
    ncols = feat // halves
    keep = ncols // 2
    piece = keep // 4
    dma = pltpu.SemaphoreType.DMA
    anywhere = pl.BlockSpec(memory_space=pl.ANY)
    vmem = pl.BlockSpec(memory_space=pltpu.VMEM)
    return pl.pallas_call(
        functools.partial(kernel, sections, dp_size, tok, feat),
        out_shape=(
            jax.ShapeDtypeStruct((CHUNKS, tok, cw), BF16),
            jax.ShapeDtypeStruct((CHUNKS, tok, cw), BF16),
            jax.ShapeDtypeStruct((8, 128), F32),
            jax.ShapeDtypeStruct((4, piece, cw), BF16),
        ),
        in_specs=[anywhere, anywhere, anywhere, vmem, vmem, vmem, anywhere],
        out_specs=(anywhere, anywhere, anywhere, anywhere),
        scratch_shapes=[
            pltpu.VMEM((feat, feat), BF16),
            pltpu.VMEM((feat, feat), BF16),
            pltpu.VMEM((micros, CHUNKS, pair, cw), BF16),
            pltpu.VMEM((micros, CHUNKS, pair, cw), BF16),
            pltpu.VMEM((micros, CHUNKS, pair, cw), BF16),
            pltpu.VMEM((pair, feat), BF16),
            pltpu.VMEM((micros, halves, pair, ncols), BF16),
            pltpu.VMEM((micros, CHUNKS, pair, cw), BF16),
            pltpu.VMEM((micros, chips, pair, ncols), BF16),
            pltpu.VMEM((micros, chips, pair, cw), BF16),
            pltpu.VMEM((micros, CHUNKS, tok, cw), F32),
            pltpu.VMEM((micros, CHUNKS, tok, cw), F32),
            pltpu.VMEM((CHUNKS, pair, cw), F32),
            pltpu.VMEM((micros, 4, tok, 128), F32),
            pltpu.VMEM((micros, 8, 128), F32),
            pltpu.VMEM((micros, 8, 128), F32),
            pltpu.VMEM((keep, cw), BF16),
            dma((CHUNKS,)),
            dma((micros,)),
            dma((micros, CHUNKS)),
            dma((micros, CHUNKS)),
            dma((micros, CHUNKS)),
            dma((micros, CHUNKS)),
            dma((micros,)),
            dma((micros,)),
            dma((micros,)),
            dma((micros,)),
            dma((CHUNKS,)),
            dma((CHUNKS,)),
            dma((micros,)),
            dma,
            dma,
            dma,
            dma((keep // 256,)),
            dma((keep // 256,)),
            dma((4,)),
            dma((4,)),
        ],
        compiler_params=pltpu.CompilerParams(
            collective_id=0, has_side_effects=True, vmem_limit_bytes=63 * 2**20
        ),
    )(*operands)


def body(
    state,
    adjoint,
    probe,
    logp,
    density_weight,
    step_size,
    norm_gain,
    norm_shift,
    branch_gate,
    weights,
):
    sections = lax.axis_size("section")
    dp_size = lax.axis_size("dp")
    section_index = lax.axis_index("section")
    micros, tok, feat = state.shape
    cw = feat // CHUNKS

    def chunked(top, low):
        both = jnp.stack([top, low.astype(BF16)], axis=1)
        shaped = both.reshape(micros, 2 * tok, CHUNKS, cw)
        return shaped.transpose(0, 2, 1, 3)

    scale = jnp.broadcast_to(-density_weight[:, :, None], (micros, 8, 128))
    top, back, div, grad = run_kernel(
        sections,
        dp_size,
        tok,
        feat,
        chunked(state, probe),
        chunked(adjoint, probe),
        scale,
        norm_gain,
        norm_shift,
        branch_gate,
        weights[0],
    )

    def own(stack):
        return lax.dynamic_index_in_dim(stack, section_index, 0, keepdims=False)

    def rows(chunks):
        return chunks.transpose(1, 0, 2).reshape(tok, feat).astype(F32)

    step_value = step_size[0]
    own_input = own(state).astype(F32)
    state_next = own_input - step_value * (rows(top) - own_input)
    own_adjoint = own(adjoint).astype(F32)
    adjoint_next = own_adjoint + step_value * (rows(back) - own_adjoint)
    divergence = jnp.sum(div) / (tok * feat)
    logp_next = own(logp)[None] + step_value * divergence
    grad_rows = grad.transpose(1, 0, 2).reshape(feat // dp_size, feat).astype(F32)
    return (state_next[None], adjoint_next[None], logp_next, grad_rows[None])


def solution(mesh):
    placed = (
        P(None, "dp", None),
        P(None, "dp", None),
        P(None, "dp", None),
        P(None, "dp"),
        P(None, "dp"),
        P(),
        P("section", None),
        P("section", None),
        P("section", None),
        P("section", None, None),
    )
    return jax.shard_map(
        body,
        mesh=mesh,
        in_specs=placed,
        out_specs=(
            P("section", "dp", None),
            P("section", "dp", None),
            P("section", "dp"),
            P("section", "dp", None),
        ),
        check_vma=False,
    )
```

time: 1170 us -> 266 us (0.23)
  starting transfers between devices: 405 us -> 0 us
  waiting for transfers between devices: 371 us -> 0 us
  Pallas kernels: 0 us -> 241 us
  matrix products: 215 us -> 0 us
  other arithmetic: 145 us -> 9.3 us
  between operations: 17.2 us -> 3.99 us
    ppermute x30 -> x0, starting transfers between devices: 405 us -> none  [the longest x15 283 us: passed_along_2(): return lax.ppermute(block, axis, route)]
    pallas_call x0 -> x1, Pallas kernels: none -> 241 us  [run_kernel(): pl.pallas_call(functools.partial(kernel, sections, dp_size, tok, feat), o...]
    reduce_scatter x1 -> x0, waiting for transfers between devices: 230 us -> none  [body(): lax.psum_scatter(lax.dot_general(left_rows, right_rows, (((0,), (0,)), ((...]
    dot_general x25 -> x0, matrix products: 215 us -> none  [the longest x16 128 us: layer_forward(): jnp.dot(normed_pair, weight_mat, preferred_element_type=jnp.float32)]
    ppermute x30 -> x0, waiting for transfers between devices: 141 us -> none  [the longest x15 99.8 us: passed_along_2(): return lax.ppermute(block, axis, route)]
    another operation x64 -> x2, other arithmetic: 56.1 us -> 2.89 us  [chunked(): both = jnp.stack([top, low.astype(BF16)], axis=1)]
    dynamic_update_slice x40 -> x0, other arithmetic: 33.8 us -> none  [put_slot(): return lax.dynamic_update_index_in_dim(stack, value, position, 0)]
    reduce_sum x57 -> x1, other arithmetic: 27.3 us -> 1.28 us  [body(): divergence = jnp.sum(div) / (tok * feat)]
  transfers between devices with their start and end apart: 31 -> 0, of which waited for: 31 -> 0; matrix products, arithmetic and copies ran while one was open for 0% -> 0% of each run, Pallas kernels for 0% -> 0%
where the time goes in v1:
time: 266 us
  Pallas kernels  241 us (91%)
  local copies, waits for them, and re-layouts  11.5 us (4%)
  other arithmetic  9.3 us (3%)
  between operations  3.99 us (2%)
    pallas_call x1, Pallas kernels, run_kernel(): pl.pallas_call(functools.partial(kernel, sections, dp_size, tok, feat), o...  241 us
    reshape x4, local copies, waits for them, and re-layouts, chunked(): shaped = both.reshape(micros, 2 * tok, CHUNKS, cw)  5.36 us

profile of v1, /device:TPU:1, one launch (start us, length us, event | category | flops | bytes accessed | tf_op | source)
XLA Modules:
  0.0 265.5 jit_solution(2365566840697061812)
XLA Ops:
  0.6 0.0 copy-start
  0.6 0.0 copy-start.3
  0.7 0.0 copy-start.4
  1.4 0.0 copy-done
  1.4 0.6 constant_dynamic-slice_fusion
  2.0 0.7 negate_bitcast_fusion
  2.7 0.7 broadcast_in_dim.2.dw_hbm
  3.4 1.5 convert_bitcast_fusion.1
  4.9 0.0 copy-done.3
  4.9 0.0 copy-done.4
  4.9 1.4 pad_maximum_fusion
  6.3 0.1 copy.17
  6.4 1.2 reshape.62
  7.7 0.0 copy-start.1
  7.7 1.5 copy.26
  9.1 0.3 copy-done.1
  9.4 0.1 copy.15
  9.6 1.2 reshape.61
  10.8 1.4 copy.27
  12.3 240.8 %shard_map.129 = (bf16[4,16,768]{2,1,0:T(8,128)(2,1)}, bf16[4,16,768]{2,1,0:T(8,128)(2,1)}, f32[8,128]{1,0:T(8,128)}, bf16[4,192,768]{2,1,0:T(8,128)(2,1)}) custom-call(bf16[8,4,32,768]{3,2,1,0:T(8,128)(2,1)} %bitcast.31, bf16[8,4,32,768]{3,2,1,0:T(8,128)(2,1)} %bitcast.30, f32[8,8,128]{2,1,0:T(8,128)} %broadcast_in_dim.2.dw_hbm, f32[1,3072]{1,0:T(1,128)} %gain_ref.1, ...), custom_call_target="tpu_custom_call" | custom-call | tf_op jit(solution)/shard_map/pallas_call | solution.py:534
  253.0 1.3 reduce_sum.9
  255.6 0.0 copy-start.2
  255.6 1.1 convert_bitcast_fusion.2
  256.7 0.1 copy.20
  256.8 0.1 reshape.64
  256.9 1.6 convert_add_fusion
  258.6 0.1 copy.19
  258.7 0.1 reshape.63
  258.8 1.6 convert_subtract_fusion.1
  260.4 0.0 copy-done.2
  260.4 0.2 convert_bitcast_fusion
  260.6 1.5 copy.22
  262.1 2.3 reshape.65
Async XLA Ops:
  0.6 0.8 copy-start
  0.6 4.3 %copy-start.3 = (bf16[8,16,3072]{2,1,0:T(8,128)(2,1)S(1)}, bf16[8,16,3072]{2,1,0:T(8,128)(2,1)}, u32[]{:S(2)}) copy-start(bf16[8,16,3072]{2,1,0:T(8,128)(2,1)} %param.11) | copy-start | bytes 2359300
  0.7 4.3 %copy-start.4 = (bf16[8,16,3072]{2,1,0:T(8,128)(2,1)S(1)}, bf16[8,16,3072]{2,1,0:T(8,128)(2,1)}, u32[]{:S(2)}) copy-start(bf16[8,16,3072]{2,1,0:T(8,128)(2,1)} %param.10) | copy-start | bytes 2359300
  7.7 1.8 copy-start.1
  255.6 4.8 %copy-start.2 = (bf16[4,192,768]{2,1,0:T(8,128)(2,1)S(1)}, bf16[4,192,768]{2,1,0:T(8,128)(2,1)}, u32[]{:S(2)}) copy-start(bf16[4,192,768]{2,1,0:T(8,128)(2,1)} %get-tuple-element.11) | copy-start | bytes 3538948

commit v2 on v1

v2 whole, which is shorter than its diff:
```python
import functools

import jax
import jax.numpy as jnp
from jax import lax
from jax.experimental import pallas as pl
from jax.experimental.pallas import tpu as pltpu
from jax.sharding import PartitionSpec as P

EPSILON = 1e-06
MESH = pl.DeviceIdType.MESH
CHUNKS = 4
LHS_ROWS = 128
ROOT_HALF = 0.7071067811865476
PHI_SCALE = 0.3989422804014327
F32 = jnp.float32
BF16 = jnp.bfloat16


def wait_bytes(ref, sem):
    pltpu.make_async_copy(ref, ref, sem).wait()


def lanes(value):
    total = value[:, 0:128]
    for at in range(128, value.shape[1], 128):
        total = total + value[:, at : at + 128]
    return total


def row_mean(value, inv):
    return jnp.sum(value, axis=1, keepdims=True) * inv


def kernel(
    sections, dp_size, tok, feat,
    state_hbm, adjoint_hbm, probe_hbm, logp_ref, dw_ref, step_ref, gain_ref, shift_ref, gate_ref, w_hbm,
    state_out, adjoint_out, logp_out, grad_out, n_hbm,
    w_vm, wt_vm, x_in, out_buf, c_in, n_buf, n_loc, g_all,
    g1_buf, g2_buf, c_buf, stats, rs_in, rs_out, signs, own_sign, own_state, own_adjoint, ex_recv, grad_acc,
    w_sem, in_sem, sign_sem, own_sem, x_ssem, x_rsem, c_ssem, c_rsem, rs_ssem, rs_rsem,
    n_ssem, n_rsem, g_ssem, g_rsem, load_sem, e_ssem, e_rsem, f_ssem, f_rsem,
):
    micros = sections
    cw = feat // CHUNKS
    pair = 2 * tok
    chips = dp_size // 2
    halves = chips // 4
    ncols = feat // halves
    keep = ncols // 2
    piece = keep // 4
    tile = keep // 2
    block_side = 256
    inv = 1.0 / feat
    half_section = sections // 2
    last = sections - 1
    spare = micros

    s = lax.axis_index("section")
    d = lax.axis_index("dp")
    core = lax.rem(d, 2)
    chip = lax.div(d, 2)
    x_at = lax.rem(chip, 2)
    d_flip = d + 2 - 4 * x_at
    my_half = lax.div(chip, 4)
    my_col = lax.rem(chip, 4)
    next_d = jnp.where(s == half_section - 1, d_flip, d)
    prev_d = jnp.where(s == half_section, d_flip, d)

    def chunk(k):
        return pl.ds(k * cw, cw)

    top = pl.ds(0, tok)
    low = pl.ds(tok, tok)
    both = pl.ds(0, pair)
    early = 256 if cw == 768 else 128
    parts = [(0, 0, early), (0, early, cw - early)] + [(k, 0, cw) for k in range(1, CHUNKS)]

    def w_copy(k):
        return pltpu.make_async_copy(w_hbm.at[:, chunk(k)], w_vm.at[:, chunk(k)], w_sem.at[k])

    def sign_copy(m):
        return pltpu.make_async_copy(probe_hbm.at[m], signs.at[m], sign_sem.at[m])

    def state_copy(m, k):
        return pltpu.make_async_copy(
            state_hbm.at[m, :, chunk(k)], x_in.at[m, k, top], in_sem.at[m, k]
        )

    own_copies = (
        pltpu.make_async_copy(state_hbm.at[s], own_state, own_sem.at[0]),
        pltpu.make_async_copy(adjoint_hbm.at[s], own_adjoint, own_sem.at[1]),
        pltpu.make_async_copy(probe_hbm.at[s], own_sign, own_sem.at[2]),
    )
    edge = (s == 0) | (s == last)

    @pl.when(edge)
    def _():
        for m in range(micros):
            sign_copy(m).start()

    @pl.when(s == 0)
    def _():
        for m in range(micros):
            for k in range(CHUNKS):
                state_copy(m, k).start()

    for k in range(CHUNKS):
        w_copy(k).start()
    for copy in own_copies:
        copy.start()
    n_buf[...] = jnp.zeros_like(n_buf)

    barrier = pltpu.get_barrier_semaphore()

    def greet_group(i, carry):
        other = lax.rem(d + i, dp_size)
        pl.semaphore_signal(barrier, inc=1, device_id=(s, other), device_id_type=MESH)
        return carry

    def greet_sections(i, carry):
        other = lax.rem(s + i, sections)
        pl.semaphore_signal(barrier, inc=1, device_id=(other, d), device_id_type=MESH)
        pl.semaphore_signal(barrier, inc=1, device_id=(other, d_flip), device_id_type=MESH)
        return carry

    lax.fori_loop(1, dp_size, greet_group, 0)
    lax.fori_loop(1, sections, greet_sections, 0)

    @pl.when(s == 0)
    def _():
        for m in range(micros):
            sign_copy(m).wait()
            for k in range(CHUNKS):
                x_in[m, k, low, :] = signs[m, :, chunk(k)].astype(BF16)

    @pl.when(s == last)
    def _():
        for m in range(micros):
            sign_copy(m).wait()
            for k in range(CHUNKS):
                out_buf[m, k, low, :] = signs[m, :, chunk(k)].astype(BF16)

    pl.semaphore_wait(barrier, dp_size - 1 + 2 * (sections - 1))

    lane = lax.broadcasted_iota(jnp.int32, (tok, 128), 1)

    def seed_copy(src, m, k, where):
        return pltpu.make_async_remote_copy(
            src_ref=src,
            dst_ref=c_in.at[m, k, where],
            send_sem=c_ssem.at[m, k],
            recv_sem=c_rsem.at[m, k],
            device_id=(s, d_flip),
            device_id_type=MESH,
        )

    def scalar_seed(m):
        return pltpu.make_async_remote_copy(
            src_ref=rs_out.at[m],
            dst_ref=rs_in.at[m],
            send_sem=rs_ssem.at[m],
            recv_sem=rs_rsem.at[m],
            device_id=(s, d_flip),
            device_id_type=MESH,
        )

    @pl.when(s == last)
    def _():
        for m in range(micros):
            weight = jnp.broadcast_to(dw_ref[m : m + 1, 0:1], (tok, 128))
            rs_out[m] = jnp.where(lane == 5, -weight, 0.0)
            scalar_seed(m).start()
            for k in range(CHUNKS):
                seed_copy(adjoint_hbm.at[m, :, chunk(k)], m, k, top).start()
                seed_copy(out_buf.at[m, k, low], m, k, low).start()

    def transpose_weights():
        count = feat // block_side

        def one(i, carry):
            at_row = pl.multiple_of(lax.div(i, count) * block_side, block_side)
            at_col = pl.multiple_of(lax.rem(i, count) * block_side, block_side)
            wt_vm[pl.ds(at_col, block_side), pl.ds(at_row, block_side)] = w_vm[
                pl.ds(at_row, block_side), pl.ds(at_col, block_side)
            ].T
            return carry

        lax.fori_loop(0, count * count, one, 0)

    @pl.when(s >= half_section)
    def _():
        for k in range(CHUNKS):
            w_copy(k).wait()
        transpose_weights()

    @pl.when(s == last)
    def _():
        for m in range(micros):
            scalar_seed(m).wait_send()
            for k in range(CHUNKS):
                wait_bytes(out_buf.at[m, k], c_ssem.at[m, k])

    def x_send(m, k, at, width):
        cols = pl.ds(at, width)
        return pltpu.make_async_remote_copy(
            src_ref=out_buf.at[m, k, both, cols],
            dst_ref=x_in.at[m, k, both, cols],
            send_sem=x_ssem.at[m, k],
            recv_sem=x_rsem.at[m, k],
            device_id=(s + 1, next_d),
            device_id_type=MESH,
        )

    def top_send(m, k, at, width):
        cols = pl.ds(at, width)
        return pltpu.make_async_remote_copy(
            src_ref=out_buf.at[m, k, top, cols],
            dst_ref=x_in.at[spare, k, top, cols],
            send_sem=x_ssem.at[m, k],
            recv_sem=x_rsem.at[spare, k],
            device_id=(m, d_flip),
            device_id_type=MESH,
        )

    def n_send(m, i):
        other = lax.rem(chip + i, chips)
        return pltpu.make_async_remote_copy(
            src_ref=n_loc.at[m, lax.div(other, 4)],
            dst_ref=n_hbm.at[m, pl.ds(chip * pair, pair)],
            send_sem=n_ssem.at[m],
            recv_sem=n_rsem.at[m],
            device_id=(s, other * 2 + core),
            device_id_type=MESH,
        )

    def n_own(m):
        return pltpu.make_async_copy(
            n_loc.at[m, my_half], n_hbm.at[m, pl.ds(chip * pair, pair)], load_sem.at[m]
        )

    def forward(m, carry):
        def rows(k):
            return x_in[m, k, top, :].astype(F32)

        def tangents(k):
            return x_in[m, k, low, :].astype(F32)

        total_u = total_w = square = cross = 0.0
        for k in range(CHUNKS):

            @pl.when(s > 0)
            def _():
                wait_bytes(x_in.at[m, k], x_rsem.at[m, k])

            u = rows(k)
            w = tangents(k)
            if k == 0:
                base_u = row_mean(lanes(u), 1.0 / cw)
                base_w = row_mean(lanes(w), 1.0 / cw)
            u = u - base_u
            w = w - base_w
            total_u = total_u + lanes(u)
            total_w = total_w + lanes(w)
            square = square + lanes(u * u)
            cross = cross + lanes(u * w)
        shift_u = row_mean(total_u, inv)
        shift_w = row_mean(total_w, inv)
        var = row_mean(square, inv) - shift_u * shift_u
        cov = row_mean(cross, inv) - shift_u * shift_w
        mean_u = base_u + shift_u
        mean_w = base_w + shift_w
        rinv = lax.rsqrt(jnp.maximum(var, 0.0) + EPSILON)
        slope = rinv * cov
        for at, value in enumerate((mean_u, mean_w, rinv, slope)):
            stats[m, at] = jnp.broadcast_to(value, (tok, 128))
        for k in range(CHUNKS):
            gain = gain_ref[:, chunk(k)]
            xhat = (rows(k) - mean_u) * rinv
            normed = xhat * gain + shift_ref[:, chunk(k)]
            normed_t = rinv * ((tangents(k) - mean_w) - xhat * slope) * gain
            n_buf[top, chunk(k)] = normed.astype(BF16)
            n_buf[low, chunk(k)] = normed_t.astype(BF16)

        for k, at, width in parts:
            cols = pl.ds(at, width)
            wide = pl.ds(k * cw + at, width)
            if at == 0:

                @pl.when((m == 0) & (s < half_section))
                def _():
                    w_copy(k).wait()

            product = jnp.dot(n_buf[...], w_vm[:, wide], preferred_element_type=F32)
            z = product[:tok]
            z_t = product[tok:pair]
            gate = gate_ref[:, wide]
            cdf = 0.5 + 0.5 * lax.erf(z * ROOT_HALF)
            zz = z * z
            pdf = PHI_SCALE * jnp.exp(-0.5 * zz)
            first = gate * (cdf + z * pdf)
            u = x_in[m, k, top, cols].astype(F32)
            w = x_in[m, k, low, cols].astype(F32)
            out_buf[m, k, top, cols] = (u + gate * (z * cdf)).astype(BF16)
            out_buf[m, k, low, cols] = (w + first * z_t).astype(BF16)

            @pl.when(s < last)
            def _():
                x_send(m, k, at, width).start()

            @pl.when(s == last)
            def _():
                top_send(m, k, at, width).start()

            g1_buf[m, k, :, cols] = first
            g2_buf[m, k, :, cols] = gate * (pdf * (2.0 - zz)) * z_t
            if k == 0 and at == 0:
                for half in range(halves):
                    n_loc[m, half] = n_buf[both, pl.ds(half * ncols, ncols)]
                for i in range(1, chips):
                    n_send(m, i).start()
                n_own(m).start()
        return carry

    @pl.when(s == 0)
    def _():
        for m in range(micros):
            for k in range(CHUNKS):
                state_copy(m, k).wait()

    lax.fori_loop(0, micros, forward, 0)

    @pl.when(s < half_section)
    def _():
        transpose_weights()

    pitch = micros * pair

    def c_out(m, k):
        return w_vm.at[pl.ds(pl.multiple_of(m * pair, pair), pair), chunk(k)]

    def g_loc(m, k):
        return w_vm.at[pl.ds(pl.multiple_of(pitch + m * pair, pair), pair), chunk(k)]

    def c_send(m, k, at, width):
        return pltpu.make_async_remote_copy(
            src_ref=c_out(m, k).at[both, pl.ds(at, width)],
            dst_ref=c_in.at[m, k, both, pl.ds(at, width)],
            send_sem=c_ssem.at[m, k],
            recv_sem=c_rsem.at[m, k],
            device_id=(s - 1, prev_d),
            device_id_type=MESH,
        )

    def back_send(m, k, at, width):
        return pltpu.make_async_remote_copy(
            src_ref=c_out(m, k).at[top, pl.ds(at, width)],
            dst_ref=c_in.at[spare, k, top, pl.ds(at, width)],
            send_sem=c_ssem.at[m, k],
            recv_sem=c_rsem.at[spare, k],
            device_id=(m, jnp.where(m == 0, d_flip, d)),
            device_id_type=MESH,
        )

    def scalar_send(m):
        slot = jnp.where(s == 0, spare, m)
        return pltpu.make_async_remote_copy(
            src_ref=rs_out.at[m],
            dst_ref=rs_in.at[slot],
            send_sem=rs_ssem.at[m],
            recv_sem=rs_rsem.at[slot],
            device_id=(
                jnp.where(s == 0, m, s - 1),
                jnp.where((s == 0) & (m == 0), d_flip, prev_d),
            ),
            device_id_type=MESH,
        )

    def g_send(m, i):
        other = lax.rem(chip + i, chips)
        cols = pl.ds(pl.multiple_of(lax.rem(other, 4) * cw, cw), cw)
        return pltpu.make_async_remote_copy(
            src_ref=w_vm.at[pl.ds(pl.multiple_of(pitch + m * pair, pair), pair), cols],
            dst_ref=g_all.at[m, chip],
            send_sem=g_ssem.at[m],
            recv_sem=g_rsem.at[m],
            device_id=(s, other * 2 + core),
            device_id_type=MESH,
        )

    def backward(m, carry):
        for k in range(CHUNKS):
            wait_bytes(c_in.at[m, k], c_rsem.at[m, k])
        wait_bytes(rs_in.at[m], rs_rsem.at[m])
        scalars = rs_in[m]
        add_u, by_u, by_w, add_t, by_t, factor, told = (scalars[:, i : i + 1] for i in range(7))
        moved = 0.0
        for k in range(CHUNKS):
            u = out_buf[m, k, top, :].astype(F32)
            w = out_buf[m, k, low, :].astype(F32)
            c = c_in[m, k, top, :].astype(F32) + (add_u + by_u * u + by_w * w)
            sign = c_in[m, k, low, :].astype(F32)
            moved = moved + lanes(sign * (w - sign))
            c_t = sign * factor + (add_t + by_t * u)
            c_buf[k, top, :] = c
            c_buf[k, low, :] = c_t
            first = g1_buf[m, k]
            n_buf[top, chunk(k)] = (c * first + c_t * g2_buf[m, k]).astype(BF16)
            n_buf[low, chunk(k)] = (c_t * first).astype(BF16)

        mean_u = stats[m, 0][:, 0:1]
        mean_w = stats[m, 1][:, 0:1]
        rinv = stats[m, 2][:, 0:1]
        slope = stats[m, 3][:, 0:1]
        square = rinv * rinv
        lean = square * slope

        sums = [0.0] * 5
        for k, at, width in parts:
            cols = pl.ds(at, width)
            wide = pl.ds(k * cw + at, width)
            product = jnp.dot(n_buf[...], wt_vm[:, wide], preferred_element_type=F32)
            gain = gain_ref[:, wide]
            a = product[:tok] * gain
            b = product[tok:pair] * gain
            out = c_out(m, k)
            out[top, cols] = (c_buf[k, top, cols] + rinv * a - lean * b).astype(BF16)
            out[low, cols] = (c_buf[k, low, cols] + rinv * b).astype(BF16)

            @pl.when(s > 0)
            def _():
                c_send(m, k, at, width).start()

            @pl.when(s == 0)
            def _():
                back_send(m, k, at, width).start()

            xhat = (x_in[m, k, top, cols].astype(F32) - mean_u) * rinv
            centered = x_in[m, k, low, cols].astype(F32) - mean_w
            for i, value in enumerate((a, a * xhat, b, b * xhat, b * centered)):
                sums[i] = sums[i] + lanes(value)
            if k == 0 and at == 0:
                for j in range(CHUNKS):
                    g_loc(m, j)[...] = n_buf[both, chunk(j)]
                for i in range(1, chips):
                    g_send(m, i).start()
        mean_a, mean_ax, mean_b, mean_bx, mean_bw = (row_mean(value, inv) for value in sums)
        beta = -rinv * mean_ax - square * (mean_bw - 3.0 * mean_bx * slope)
        gamma = -square * mean_bx
        alpha = lean * mean_b - rinv * mean_a
        values = (
            alpha - beta * rinv * mean_u - gamma * mean_w,
            beta * rinv,
            gamma,
            -rinv * mean_b - gamma * mean_u,
            gamma,
            1.0,
            jnp.where(s == last, jnp.sum(moved, axis=1, keepdims=True), told),
        )
        packed = 0.0
        for at, value in enumerate(values):
            packed = jnp.where(lane == at, value, packed)
        rs_out[m] = packed
        scalar_send(m).start()
        g_all[m, chip] = own_block(m)
        return carry

    def own_block(m):
        cols = pl.ds(pl.multiple_of(my_col * cw, cw), cw)
        return w_vm[pl.ds(pl.multiple_of(pitch + m * pair, pair), pair), cols]

    lax.fori_loop(0, micros, backward, 0)

    base = 2 * pitch
    depth = chips * pair

    def n_load(m):
        return pltpu.make_async_copy(
            n_hbm.at[m], w_vm.at[pl.ds(base + m * depth, depth), pl.ds(0, ncols)], load_sem.at[m]
        )

    for m in range(micros):
        n_own(m).wait()
        wait_bytes(n_hbm.at[m, pl.ds(0, depth - pair)], n_rsem.at[m])
        n_load(m).start()
    spot = base if halves > 1 else base + micros * depth
    ex_send = w_vm.at[pl.ds(spot, keep), pl.ds(feat // 2, cw)]
    fin_send = w_vm.at[pl.ds(spot, keep), pl.ds(feat // 2 + cw, cw)]
    most = micros * 3 // 4

    def block(start, first, count):
        cols = pl.ds(pl.multiple_of(start, 128), tile)
        left = w_vm[pl.ds(base + first * depth, count * depth), cols]
        right = g_all[pl.ds(first, count)].reshape(count * depth, cw)
        return lax.dot_general(left, right, (((0,), (0,)), ((), ())), preferred_element_type=F32)

    def gathered(first, count):
        for m in range(first, first + count):
            wait_bytes(g_all.at[m, pl.ds(0, chips - 1)], g_rsem.at[m])
            n_load(m).wait()

    starts = [(1 - core) * keep, (1 - core) * keep + tile, core * keep, core * keep + tile]
    gathered(0, most)
    for i in range(4):
        grad_acc[i] = block(starts[i], 0, most)
    gathered(most, micros - most)

    def ex_copy(i):
        at = pl.ds(i * tile, tile)
        return pltpu.make_async_remote_copy(
            src_ref=ex_send.at[at],
            dst_ref=ex_recv.at[at],
            send_sem=e_ssem.at[i],
            recv_sem=e_rsem.at[i],
            device_id=(s, d + 1 - 2 * core),
            device_id_type=MESH,
        )

    goal = (2 * my_half + core) * 4
    grad_cols = pl.ds(pl.multiple_of(my_col * cw, cw), cw)

    def piece_send(j):
        return pltpu.make_async_remote_copy(
            src_ref=fin_send.at[pl.ds(j * piece, piece)],
            dst_ref=grad_out.at[:, grad_cols],
            send_sem=f_ssem.at[j],
            recv_sem=f_rsem.at[my_col],
            device_id=(s, goal + j),
            device_id_type=MESH,
        )

    def piece_own(j):
        return pltpu.make_async_copy(
            fin_send.at[pl.ds(j * piece, piece)], grad_out.at[:, grad_cols], f_rsem.at[my_col]
        )

    for i in range(2):
        ex_send[pl.ds(i * tile, tile), :] = (
            grad_acc[i] + block(starts[i], most, micros - most)
        ).astype(BF16)
        ex_copy(i).start()
    for i in range(2):
        at = pl.ds(i * tile, tile)
        mine = grad_acc[2 + i] + block(starts[2 + i], most, micros - most)
        wait_bytes(ex_recv.at[at], e_rsem.at[i])
        fin_send[at, :] = (mine + ex_recv[at, :].astype(F32)).astype(BF16)
        for j in (2 * i, 2 * i + 1):

            @pl.when(goal + j != d)
            def _():
                piece_send(j).start()

            @pl.when(goal + j == d)
            def _():
                piece_own(j).start()

    for copy in own_copies:
        copy.wait()
    for k in range(CHUNKS):
        wait_bytes(x_in.at[spare, k, top], x_rsem.at[spare, k])
        wait_bytes(c_in.at[spare, k, top], c_rsem.at[spare, k])
    wait_bytes(rs_in.at[spare], rs_rsem.at[spare])
    step = step_ref[...]
    scalars = jnp.where(s == 0, rs_out[0], rs_in[spare])
    for k in range(CHUNKS):
        sign = own_sign[:, chunk(k)].astype(F32)
        start = own_state[:, chunk(k)].astype(F32)
        first = own_adjoint[:, chunk(k)].astype(F32)
        final_u = x_in[spare, k, top, :].astype(F32)
        state_out[:, chunk(k)] = start - step * (final_u - start)
        back = jnp.where(s == 0, c_out(0, k)[top, :].astype(F32), c_in[spare, k, top, :].astype(F32))
        back = back + (scalars[:, 0:1] + scalars[:, 1:2] * start + scalars[:, 2:3] * sign)
        adjoint_out[:, chunk(k)] = first + step * (back - first)
    summed = jnp.sum(scalars[:, 6:7], axis=0, keepdims=True)
    which = lax.broadcasted_iota(jnp.int32, (micros, 1), 0)
    mine = jnp.sum(jnp.where(which == s, logp_ref[...], 0.0), axis=0, keepdims=True)
    logp_out[...] = mine + step * (summed / (tok * feat))

    def drain(m, carry):
        wait_bytes(n_hbm.at[m, pl.ds(0, depth - pair)], n_ssem.at[m])
        wait_bytes(g_all.at[m, pl.ds(0, chips - 1)], g_ssem.at[m])
        scalar_send(m).wait_send()

        @pl.when(s < last)
        def _():
            for k in range(CHUNKS):
                wait_bytes(out_buf.at[m, k], x_ssem.at[m, k])

        @pl.when(s == last)
        def _():
            for k in range(CHUNKS):
                wait_bytes(out_buf.at[m, k, top], x_ssem.at[m, k])

        @pl.when(s > 0)
        def _():
            for k in range(CHUNKS):
                wait_bytes(c_in.at[m, k], c_ssem.at[m, k])

        @pl.when(s == 0)
        def _():
            for k in range(CHUNKS):
                wait_bytes(c_in.at[m, k, top], c_ssem.at[m, k])

        return carry

    lax.fori_loop(0, micros, drain, 0)
    for i in range(2):
        ex_copy(i).wait_send()
    for j in range(4):

        @pl.when(goal + j != d)
        def _():
            piece_send(j).wait_send()

        wait_bytes(grad_out.at[:, chunk(j)], f_rsem.at[j])


def run_kernel(sections, dp_size, tok, feat, *operands):
    micros = sections
    cw = feat // CHUNKS
    pair = 2 * tok
    chips = dp_size // 2
    halves = chips // 4
    ncols = feat // halves
    keep = ncols // 2
    piece = keep // 4
    dma = pltpu.SemaphoreType.DMA
    anywhere = pl.BlockSpec(memory_space=pl.ANY)
    vmem = pl.BlockSpec(memory_space=pltpu.VMEM)
    return pl.pallas_call(
        functools.partial(kernel, sections, dp_size, tok, feat),
        out_shape=(
            jax.ShapeDtypeStruct((tok, feat), F32),
            jax.ShapeDtypeStruct((tok, feat), F32),
            jax.ShapeDtypeStruct((1, 1), F32),
            jax.ShapeDtypeStruct((piece, feat), BF16),
            jax.ShapeDtypeStruct((micros, chips * pair, ncols), BF16),
        ),
        in_specs=[anywhere] * 3 + [vmem] * 6 + [anywhere],
        out_specs=(vmem, vmem, vmem, anywhere, anywhere),
        scratch_shapes=[
            pltpu.VMEM((feat, feat), BF16),
            pltpu.VMEM((feat, feat), BF16),
            pltpu.VMEM((micros + 1, CHUNKS, pair, cw), BF16),
            pltpu.VMEM((micros, CHUNKS, pair, cw), BF16),
            pltpu.VMEM((micros + 1, CHUNKS, pair, cw), BF16),
            pltpu.VMEM((LHS_ROWS, feat), BF16),
            pltpu.VMEM((micros, halves, pair, ncols), BF16),
            pltpu.VMEM((micros, chips, pair, cw), BF16),
            pltpu.VMEM((micros, CHUNKS, tok, cw), F32),
            pltpu.VMEM((micros, CHUNKS, tok, cw), F32),
            pltpu.VMEM((CHUNKS, pair, cw), F32),
            pltpu.VMEM((micros, 4, tok, 128), F32),
            pltpu.VMEM((micros + 1, tok, 128), F32),
            pltpu.VMEM((micros, tok, 128), F32),
            pltpu.VMEM((micros, tok, feat), jnp.int32),
            pltpu.VMEM((tok, feat), jnp.int32),
            pltpu.VMEM((tok, feat), BF16),
            pltpu.VMEM((tok, feat), BF16),
            pltpu.VMEM((keep, cw), BF16),
            pltpu.VMEM((4, keep // 2, cw), F32),
            dma((CHUNKS,)),
            dma((micros, CHUNKS)),
            dma((micros,)),
            dma((3,)),
            dma((micros, CHUNKS)),
            dma((micros + 1, CHUNKS)),
            dma((micros, CHUNKS)),
            dma((micros + 1, CHUNKS)),
            dma((micros,)),
            dma((micros + 1,)),
            dma((micros,)),
            dma((micros,)),
            dma((micros,)),
            dma((micros,)),
            dma((micros,)),
            dma((2,)),
            dma((2,)),
            dma((4,)),
            dma((4,)),
        ],
        compiler_params=pltpu.CompilerParams(
            collective_id=0, has_side_effects=True, vmem_limit_bytes=63 * 2**20
        ),
    )(*operands)


def body(
    state,
    adjoint,
    probe,
    logp,
    density_weight,
    step_size,
    norm_gain,
    norm_shift,
    branch_gate,
    weights,
):
    _, tok, feat = state.shape
    state_next, adjoint_next, logp_next, grad, _ = run_kernel(
        lax.axis_size("section"),
        lax.axis_size("dp"),
        tok,
        feat,
        state,
        adjoint,
        probe,
        logp,
        density_weight,
        step_size[None],
        norm_gain,
        norm_shift,
        branch_gate,
        weights[0],
    )
    return (state_next[None], adjoint_next[None], logp_next, grad[None].astype(F32))


def solution(mesh):
    placed = (
        P(None, "dp", None),
        P(None, "dp", None),
        P(None, "dp", None),
        P(None, "dp"),
        P(None, "dp"),
        P(),
        P("section", None),
        P("section", None),
        P("section", None),
        P("section", None, None),
    )
    return jax.shard_map(
        body,
        mesh=mesh,
        in_specs=placed,
        out_specs=(
            P("section", "dp", None),
            P("section", "dp", None),
            P("section", "dp"),
            P("section", "dp", None),
        ),
        check_vma=False,
    )
```

time: 266 us -> 235 us (0.88)
  Pallas kernels: 241 us -> 225 us
  local copies, waits for them, and re-layouts: 11.5 us -> 4 us
  other arithmetic: 9.3 us -> 2.99 us
    pallas_call x1, Pallas kernels: 241 us -> 225 us  [run_kernel(): pl.pallas_call(functools.partial(kernel, sections, dp_size, tok, feat), o...]
    reshape x4 -> x0, local copies, waits for them, and re-layouts: 5.36 us -> none  [chunked(): shaped = both.reshape(micros, 2 * tok, CHUNKS, cw)]
    convert_element_type x6 -> x0, local copies, waits for them, and re-layouts: 4.24 us -> none  [the longest x2 3.78 us: body(): grad.transpose(1, 0, 2).reshape(feat // dp_size, feat).astype(F32)]
    unnamed x10 -> x8, local copies, waits for them, and re-layouts: 0.33 us -> 4 us
    another operation x2 -> x0, other arithmetic: 2.89 us -> none  [chunked(): both = jnp.stack([top, low.astype(BF16)], axis=1)]
where the time goes in v2:
time: 235 us
  Pallas kernels  225 us (96%)
  local copies, waits for them, and re-layouts  4 us (2%)
  between operations  3.12 us (1%)
  other arithmetic  2.99 us (1%)
    pallas_call x1, Pallas kernels, run_kernel(): pl.pallas_call(functools.partial(kernel, sections, dp_size, tok, feat), o...  225 us

profile of v2, /device:TPU:1, one launch (start us, length us, event | category | flops | bytes accessed | tf_op | source)
XLA Modules:
  0.0 235.2 jit_solution(8915615868799858943)
XLA Ops:
  1.3 1.3 copy.14.logp_ref
  2.6 1.3 copy.15.dw_ref
  3.9 225.1 %shard_map.129 = (f32[16,3072]{1,0:T(8,128)}, f32[16,3072]{1,0:T(8,128)}, f32[1,1]{1,0:T(1,128)}, bf16[192,3072]{1,0:T(8,128)(2,1)}, bf16[8,256,1536]{2,1,0:T(8,128)(2,1)}) custom-call(bf16[8,16,3072]{2,1,0:T(8,128)(2,1)} %state_hbm.1, bf16[8,16,3072]{2,1,0:T(8,128)(2,1)} %adjoint_hbm.1, s32[8,16,3072]{2,1,0:T(8,128)} %probe_hbm.1, f32[8,1]{1,0:T(8,128)} %copy.14.logp_ref, ...), custom_call_target="tpu_custom_call" | custom-call | tf_op jit(solution)/shard_map/pallas_call | solution.py:630
  229.1 0.0 copy-start.1
  229.1 0.0 copy-start
  229.1 3.0 %bitcast_convert_fusion = f32[1,192,3072]{2,1,0:T(8,128)} fusion(bf16[192,3072]{1,0:T(8,128)(2,1)} %get-tuple-element.11), kind=kLoop, calls=%fused_computation | loop fusion | flops 589824 | bytes 3538944 | tf_op jit(solution)/shard_map/convert_element_type | solution.py:717
  232.1 0.0 copy-done.1
  232.1 0.7 copy.20
  232.7 0.0 copy-done
  232.7 0.7 copy.21
Async XLA Ops:
  229.1 3.0 %copy-start.1 = (f32[16,3072]{1,0:T(8,128)S(1)}, f32[16,3072]{1,0:T(8,128)}, u32[]{:S(2)}) copy-start(f32[16,3072]{1,0:T(8,128)} %get-tuple-element.8) | copy-start | bytes 589828
  229.1 3.7 %copy-start = (f32[16,3072]{1,0:T(8,128)S(1)}, f32[16,3072]{1,0:T(8,128)}, u32[]{:S(2)}) copy-start(f32[16,3072]{1,0:T(8,128)} %get-tuple-element.9) | copy-start | bytes 589828

commit v3 on v2

--- a/solution.py
+++ b/solution.py
@@ -61,7 +61,7 @@
     core = lax.rem(d, 2)
     chip = lax.div(d, 2)
     x_at = lax.rem(chip, 2)
-    d_flip = d + 2 - 4 * x_at
+    d_flip = d + 2 - 4 * x_at + 1 - 2 * core
     my_half = lax.div(chip, 4)
     my_col = lax.rem(chip, 4)
     next_d = jnp.where(s == half_section - 1, d_flip, d)
@@ -168,7 +168,7 @@
     @pl.when(s == last)
     def _():
         for m in range(micros):
-            weight = jnp.broadcast_to(dw_ref[m : m + 1, 0:1], (tok, 128))
+            weight = jnp.broadcast_to(dw_ref[0:1, m : m + 1], (tok, 128))
             rs_out[m] = jnp.where(lane == 5, -weight, 0.0)
             scalar_seed(m).start()
             for k in range(CHUNKS):
@@ -572,8 +572,8 @@
         back = back + (scalars[:, 0:1] + scalars[:, 1:2] * start + scalars[:, 2:3] * sign)
         adjoint_out[:, chunk(k)] = first + step * (back - first)
     summed = jnp.sum(scalars[:, 6:7], axis=0, keepdims=True)
-    which = lax.broadcasted_iota(jnp.int32, (micros, 1), 0)
-    mine = jnp.sum(jnp.where(which == s, logp_ref[...], 0.0), axis=0, keepdims=True)
+    which = lax.broadcasted_iota(jnp.int32, (1, micros), 1)
+    mine = jnp.sum(jnp.where(which == s, logp_ref[...], 0.0), axis=1, keepdims=True)
     logp_out[...] = mine + step * (summed / (tok * feat))
 
     def drain(m, carry):
@@ -706,8 +706,8 @@
         state,
         adjoint,
         probe,
-        logp,
-        density_weight,
+        logp.reshape(1, -1),
+        density_weight.reshape(1, -1),
         step_size[None],
         norm_gain,
         norm_shift,

time: 235 us -> 234 us (level)
  local copies, waits for them, and re-layouts: 4 us -> 1.36 us
    unnamed x8 -> x6, local copies, waits for them, and re-layouts: 4 us -> 1.36 us
where the time goes in v3:
time: 234 us
  Pallas kernels  226 us (97%)
  between operations  3.12 us (1%)
  other arithmetic  2.99 us (1%)
    pallas_call x1, Pallas kernels, run_kernel(): pl.pallas_call(functools.partial(kernel, sections, dp_size, tok, feat), o...  226 us

profile of v3, /device:TPU:1, one launch (start us, length us, event | category | flops | bytes accessed | tf_op | source)
XLA Modules:
  0.0 233.9 jit_solution(8523121363839686117)
XLA Ops:
  1.3 226.4 %shard_map.129 = (f32[16,3072]{1,0:T(8,128)}, f32[16,3072]{1,0:T(8,128)}, f32[1,1]{1,0:T(1,128)}, bf16[192,3072]{1,0:T(8,128)(2,1)}, bf16[8,256,1536]{2,1,0:T(8,128)(2,1)}) custom-call(bf16[8,16,3072]{2,1,0:T(8,128)(2,1)} %state_hbm.1, bf16[8,16,3072]{2,1,0:T(8,128)(2,1)} %adjoint_hbm.1, s32[8,16,3072]{2,1,0:T(8,128)} %probe_hbm.1, f32[1,8]{1,0:T(1,128)} %bitcast.13, ...), custom_call_target="tpu_custom_call" | custom-call | tf_op jit(solution)/shard_map/pallas_call | solution.py:630
  227.7 0.0 copy-start.1
  227.7 0.0 copy-start
  227.7 3.0 %bitcast_convert_fusion = f32[1,192,3072]{2,1,0:T(8,128)} fusion(bf16[192,3072]{1,0:T(8,128)(2,1)} %get-tuple-element.11), kind=kLoop, calls=%fused_computation | loop fusion | flops 589824 | bytes 3538944 | tf_op jit(solution)/shard_map/convert_element_type | solution.py:717
  230.7 0.0 copy-done.1
  230.7 0.7 copy.18
  231.4 0.0 copy-done
  231.4 0.7 copy.19
Async XLA Ops:
  227.7 3.0 %copy-start.1 = (f32[16,3072]{1,0:T(8,128)S(1)}, f32[16,3072]{1,0:T(8,128)}, u32[]{:S(2)}) copy-start(f32[16,3072]{1,0:T(8,128)} %get-tuple-element.8) | copy-start | bytes 589828
  227.7 3.7 %copy-start = (f32[16,3072]{1,0:T(8,128)S(1)}, f32[16,3072]{1,0:T(8,128)}, u32[]{:S(2)}) copy-start(f32[16,3072]{1,0:T(8,128)} %get-tuple-element.9) | copy-start | bytes 589828

commit v4 on v3

--- a/solution.py
+++ b/solution.py
@@ -486,7 +486,7 @@
     spot = base if halves > 1 else base + micros * depth
     ex_send = w_vm.at[pl.ds(spot, keep), pl.ds(feat // 2, cw)]
     fin_send = w_vm.at[pl.ds(spot, keep), pl.ds(feat // 2 + cw, cw)]
-    most = micros * 3 // 4
+    most = micros - 1
 
     def block(start, first, count):
         cols = pl.ds(pl.multiple_of(start, 128), tile)
@@ -506,7 +506,7 @@
     gathered(most, micros - most)
 
     def ex_copy(i):
-        at = pl.ds(i * tile, tile)
+        at = pl.ds(pl.multiple_of(i * tile, tile), tile)
         return pltpu.make_async_remote_copy(
             src_ref=ex_send.at[at],
             dst_ref=ex_recv.at[at],
@@ -521,7 +521,7 @@
 
     def piece_send(j):
         return pltpu.make_async_remote_copy(
-            src_ref=fin_send.at[pl.ds(j * piece, piece)],
+            src_ref=fin_send.at[pl.ds(pl.multiple_of(j * piece, 16), piece)],
             dst_ref=grad_out.at[:, grad_cols],
             send_sem=f_ssem.at[j],
             recv_sem=f_rsem.at[my_col],
@@ -531,20 +531,22 @@
 
     def piece_own(j):
         return pltpu.make_async_copy(
-            fin_send.at[pl.ds(j * piece, piece)], grad_out.at[:, grad_cols], f_rsem.at[my_col]
-        )
-
-    for i in range(2):
-        ex_send[pl.ds(i * tile, tile), :] = (
-            grad_acc[i] + block(starts[i], most, micros - most)
-        ).astype(BF16)
-        ex_copy(i).start()
-    for i in range(2):
-        at = pl.ds(i * tile, tile)
-        mine = grad_acc[2 + i] + block(starts[2 + i], most, micros - most)
-        wait_bytes(ex_recv.at[at], e_rsem.at[i])
+            fin_send.at[pl.ds(pl.multiple_of(j * piece, 16), piece)], grad_out.at[:, grad_cols], f_rsem.at[my_col]
+        )
+
+    order = (1 - x_at, x_at)
+
+    for t in order:
+        late = block((1 - core) * keep + t * tile, most, micros - most)
+        at = pl.ds(pl.multiple_of(t * tile, tile), tile)
+        ex_send[at, :] = (grad_acc[t] + late).astype(BF16)
+        ex_copy(t).start()
+    for t in order:
+        at = pl.ds(pl.multiple_of(t * tile, tile), tile)
+        mine = grad_acc[2 + t] + block(core * keep + t * tile, most, micros - most)
+        wait_bytes(ex_recv.at[at], e_rsem.at[t])
         fin_send[at, :] = (mine + ex_recv[at, :].astype(F32)).astype(BF16)
-        for j in (2 * i, 2 * i + 1):
+        for j in (2 * t, 2 * t + 1):
 
             @pl.when(goal + j != d)
             def _():

time: 234 us -> 233 us (level)
  no operation moved by 1% of the time
where the time goes in v4:
time: 233 us
  Pallas kernels  226 us (97%)
  between operations  3.12 us (1%)
  other arithmetic  2.99 us (1%)
    pallas_call x1, Pallas kernels, run_kernel(): pl.pallas_call(functools.partial(kernel, sections, dp_size, tok, feat), o...  226 us

profile of v4, /device:TPU:1, one launch (start us, length us, event | category | flops | bytes accessed | tf_op | source)
XLA Modules:
  0.0 233.1 jit_solution(16442596161070483660)
XLA Ops:
  1.3 225.7 %shard_map.129 = (f32[16,3072]{1,0:T(8,128)}, f32[16,3072]{1,0:T(8,128)}, f32[1,1]{1,0:T(1,128)}, bf16[192,3072]{1,0:T(8,128)(2,1)}, bf16[8,256,1536]{2,1,0:T(8,128)(2,1)}) custom-call(bf16[8,16,3072]{2,1,0:T(8,128)(2,1)} %state_hbm.1, bf16[8,16,3072]{2,1,0:T(8,128)(2,1)} %adjoint_hbm.1, s32[8,16,3072]{2,1,0:T(8,128)} %probe_hbm.1, f32[1,8]{1,0:T(1,128)} %bitcast.13, ...), custom_call_target="tpu_custom_call" | custom-call | tf_op jit(solution)/shard_map/pallas_call | solution.py:632
  227.0 0.0 copy-start.1
  227.0 0.0 copy-start
  227.0 3.0 %bitcast_convert_fusion = f32[1,192,3072]{2,1,0:T(8,128)} fusion(bf16[192,3072]{1,0:T(8,128)(2,1)} %get-tuple-element.11), kind=kLoop, calls=%fused_computation | loop fusion | flops 589824 | bytes 3538944 | tf_op jit(solution)/shard_map/convert_element_type | solution.py:719
  230.0 0.0 copy-done.1
  230.0 0.7 copy.18
  230.7 0.0 copy-done
  230.7 0.7 copy.19
Async XLA Ops:
  227.0 3.0 %copy-start.1 = (f32[16,3072]{1,0:T(8,128)S(1)}, f32[16,3072]{1,0:T(8,128)}, u32[]{:S(2)}) copy-start(f32[16,3072]{1,0:T(8,128)} %get-tuple-element.8) | copy-start | bytes 589828
  227.0 3.7 %copy-start = (f32[16,3072]{1,0:T(8,128)S(1)}, f32[16,3072]{1,0:T(8,128)}, u32[]{:S(2)}) copy-start(f32[16,3072]{1,0:T(8,128)} %get-tuple-element.9) | copy-start | bytes 589828
